TPU v7x, 32 devices: a whole 2x2x4 slice. The times are simulated.
32 devices in a mesh: slab: 4 (over y, x), energy: 8 (over z, core).
Axes of the slice: x: 2, y: 2, z: 4, core: 2. Of those that a mesh axis runs over, the one named last changes fastest.
Arguments:
- link_p: float32 [12, 2, 64, 64], P('slab'), may hold values from -1 to 2, as said below
- link_q: float32 [12, 2, 64, 64], P('slab'), may hold values from -1 to 2, as said below
- shift: float32 [64, 12, 64], P('energy', 'slab'), may hold values from 0.01 to 0.3
- lesser_gain: float32 [64, 12, 64], P('energy', 'slab'), may hold values from 0.1 to 2
- sources: float32 [12, 2, 64, 128], P('slab'), may hold values from -1.8 to 1.8
Outputs:
- polar: float32 [2, 64, 12, 64, 128], P(None, None, 'slab', 'energy')
Inputs may be any that keep to these rules, and one draw needn't show every extreme that they name: `link_p`: real and imaginary parts of complex link factors. `link_q`: real and imaginary parts of complex link factors.
All inputs are finite; a program needn't handle non-finite values.
Results may differ from a plain program's by a relative error of at most 0.0003.
Values sent between devices are 32-bit elements; how exact they have to be, the bound alone decides.
No kernel may reach another device: no remote copies, remote signals or barrier semaphores. Data moves between devices by JAX's collectives and lax.ppermute only.
A program may use at most 128 MiB of HBM per device.

v0:
```python
import functools

import jax
import jax.numpy as jnp
from jax import lax
from jax.experimental import pallas as pl
from jax.experimental.pallas import tpu as pltpu
from jax.sharding import PartitionSpec as P

F32 = jnp.float32
BF16 = jnp.bfloat16
VMEM_LIMIT = 56 * 1024 * 1024
LEAST = 0.0095
CLOSE = 1e-3
STRIDE = 4
GROUP = 12
HALVES = 2


def elimination_levels(count):
    levels = []
    chain = list(range(count))
    while len(chain) > 1:
        level = []
        for place in range(0, len(chain), 2):
            left = chain[place - 1] if place > 0 else None
            right = chain[place + 1] if place + 1 < len(chain) else None
            level.append((chain[place], left, right))
        levels.append(level)
        chain = chain[1::2]
    return levels, chain[0]


def split(x, count):
    parts = []
    for place in range(count):
        part = x.astype(BF16)
        parts.append(part)
        if place + 1 < count:
            x = x - part.astype(F32)
    return parts


def half_roll(x):
    return pltpu.roll(x, x.shape[1] // 2, 1)


def turned(block, count):
    half = block.shape[1] // 2
    top = split(block, count)
    if half % 128 == 0:
        bottom = [jnp.concatenate([-part[:, half:], part[:, :half]], axis=1) for part in top]
    else:
        low = lax.broadcasted_iota(jnp.int32, block.shape, 1) < half
        rolled = half_roll(block)
        bottom = split(jnp.where(low, -rolled, rolled), count)
    return [jnp.concatenate([one, two], axis=0) for one, two in zip(top, bottom)]


def wide(x):
    half = x.shape[0] // 2
    return jnp.concatenate([x[:half], x[half:]], axis=1)


def tall(x):
    half = x.shape[1] // 2
    return jnp.concatenate([x[:, :half], x[:, half:]], axis=0)


def above(blocks, count):
    parts = [turned(block, count) for block in blocks]
    if len(parts) == 1:
        return parts[0]
    return [jnp.concatenate([part[k] for part in parts], axis=0) for k in range(count)]


def times(a, right, contract=0):
    left = split(a, len(right))
    if len(right) == 3:
        left = [left[0], left[1], left[0], left[1], left[0], left[2]]
        right = [right[0], right[0], right[1], right[1], right[2], right[0]]
    else:
        left = [left[0], left[1], left[0]]
        right = [right[0], right[0], right[1]]
    return lax.dot_general(
        jnp.concatenate(left, axis=1),
        jnp.concatenate(right, axis=contract),
        (((1,), (contract,)), ((), ())),
        preferred_element_type=F32,
    )


def over_energies(mine, many, work):
    if many and mine > 2 and mine % 2 == 0:

        def two(place, unused):
            work([2 * place, 2 * place + 1])
            return 0

        lax.fori_loop(0, mine // 2, two, 0)
    else:
        work(list(range(mine)))


def invert_batch(mat_ref, inv_ref, near_ref, first, number, top):
    size = next(size for size in range(min(number, GROUP), 0, -1) if number % size == 0)
    if size == number:
        invert_group(mat_ref, inv_ref, near_ref, range(first, first + number), top)
    else:

        def group(place, unused):
            begin = first + place * size
            invert_group(mat_ref, inv_ref, near_ref, [begin + n for n in range(size)], top)
            return 0

        lax.fori_loop(0, number // size, group, 0)


def invert_group(mat_ref, inv_ref, near_ref, members, top):
    shape = mat_ref.shape[1:]
    count = shape[0]
    lane = lax.broadcasted_iota(jnp.int32, shape, 1)
    sub = lax.broadcasted_iota(jnp.int32, shape, 0)
    eye = jnp.where(lane == sub, 1.0, 0.0).astype(F32)
    total = top + LEAST

    def factor_of(reach):
        squared = reach * reach
        gain = 2.0 / (2.0 - squared)
        return gain, 0.5 * squared * gain

    def pair_step(unused, reach):
        gain, after = factor_of(reach)
        ts = [near_ref[m] for m in members]
        both = [jnp.concatenate([inv_ref[m], t], axis=0) for m, t in zip(members, ts)]
        pairs = [times(x, turned((2.0 * eye - t) * gain, 2)) for x, t in zip(both, ts)]
        for m, pair in zip(members, pairs):
            inv_ref[m] = pair[:count]
            near_ref[m] = pair[count:]
        return after

    def cycle(state):
        number, reach = state
        reach = lax.fori_loop(0, number, pair_step, reach)
        gain, after = factor_of(reach)
        xs = [times(inv_ref[m], turned((2.0 * eye - near_ref[m]) * gain, 2)) for m in members]
        for m, x in zip(members, xs):
            inv_ref[m] = x

        @pl.when(after > CLOSE)
        def _():
            ts = [times(mat_ref[m], turned(inv_ref[m], 2)) for m in members]
            for m, t in zip(members, ts):
                near_ref[m] = t

        return jnp.int32(STRIDE - 1), after

    start = 2.0 / total
    gain, reach = factor_of((top - LEAST) / total)
    ts = [mat_ref[m] * start for m in members]
    bases = [(2.0 * eye - t) * gain for t in ts]
    products = [times(t, turned(base, 2)) for t, base in zip(ts, bases)]
    for m, base, product in zip(members, bases, products):
        inv_ref[m] = base * start
        near_ref[m] = product
    lax.while_loop(lambda state: state[1] > CLOSE, cycle, (jnp.int32(STRIDE - 2), reach))
    xs = [inv_ref[m] for m in members]
    rests = [eye - times(mat_ref[m], turned(x, 3)) for m, x in zip(members, xs)]
    for m, x, rest in zip(members, xs, rests):
        inv_ref[m] = x + times(x, turned(rest, 2))


def slots(levels, root):
    order = [node for level in levels for node, _, _ in level] + [root]
    return {node: place for place, node in enumerate(order)}


def link_places(slabs, mine, levels):
    places = {}
    for s in range(slabs - 1):
        for e in range(mine):
            places[(0, s, s + 1, e)] = (True, s)
    spare = 0
    for depth, level in enumerate(levels):
        for node, left, right in level:
            if left is not None and right is not None:
                for e in range(mine):
                    places[(depth + 1, left, right, e)] = (False, spare)
                    spare += 1
    return places, spare


def climb(levels, spot, mine, w1, w2, sol, finished):
    for level in reversed(levels):

        def work(energies, level=level):
            values = []
            for node, left, right in level:
                for e in energies:
                    m = spot[node] * mine + e
                    steps, sides = [], []
                    if left is not None:
                        steps.append(w1[m])
                        sides.append(wide(sol[spot[left] * mine + e]))
                    if right is not None:
                        steps.append(w2[m])
                        sides.append(wide(sol[spot[right] * mine + e]))
                    steps = steps[0] if len(steps) == 1 else jnp.concatenate(steps, axis=1)
                    values.append((m, sol[m] - tall(times(steps, above(sides, 2)))))
            for m, value in values:
                sol[m] = value

        over_energies(mine, len(level) > 2, work)
        finished([node for node, _, _ in level])


def orbitals_of(ref, m, half, halves, orbits):
    count = orbits // halves
    found = [ref[m, 0:count, :], ref[m, orbits : orbits + count, :]]
    for h in range(1, halves):
        found = [
            jnp.where(half == h, ref[m, low + h * count : low + (h + 1) * count, :], kept)
            for low, kept in zip((0, orbits), found)
        ]
    return found


def retarded_kernel(plan, where_ref, *refs):
    (slabs, mine, orbits, groups, halves, lines, per, orb_per) = plan
    factors_ref, src_ref = refs[:2]
    own_settings = refs[2 : 2 + halves]
    refs = refs[2 + halves :]
    peers = refs[: 2 * (groups - 1)]
    refs = refs[2 * (groups - 1) :]
    local = own_settings[0].shape[1]
    power_ref, gains, outs = refs[0], refs[1], refs[2:10]
    inv, w1, w2, up1, dn1, up2, dn2, sol, data, mat, rhs, near, sems = refs[10:]
    stores = (inv, w1, w2, up1, dn1, up2, dn2, sol)
    copies = []

    def copy_out(which, low_place, high_place):
        part = pl.ds(low_place, high_place - low_place)
        copy = pltpu.make_async_copy(stores[which].at[part], outs[which].at[part], sems.at[len(copies)])
        copy.start()
        copies.append(copy)

    width = 2 * orbits
    columns = src_ref.shape[-1]
    share = mine // halves
    levels, root = elimination_levels(slabs)
    spot = slots(levels, root)
    places, _ = link_places(slabs, mine, levels)
    lane = lax.broadcasted_iota(jnp.int32, (orbits, width), 1)
    sub = lax.broadcasted_iota(jnp.int32, (orbits, width), 0)
    diag_lane = lane == sub
    first, owner, core, half = where_ref[0], where_ref[1], where_ref[2], where_ref[3]

    for i in range(per):
        at = owner * per + i
        data[at, 0:width, :] = factors_ref[i]
        data[at, width : width + orbits, :] = src_ref[i, 0]
        data[at, width + orbits : 2 * width, :] = src_ref[i, 1]
        for h in range(halves):
            data[at, 2 * width + h * local : 2 * width + (h + 1) * local, :] = own_settings[h][i]
    for k in range(1, groups):
        mine_half, other_half = peers[2 * (k - 1)], peers[2 * (k - 1) + 1]
        for i in range(per):
            at = (owner ^ k) * per + i
            data[at, pl.ds(pl.multiple_of(core * width, width), width), :] = mine_half[i, 0:width, :]
            data[at, pl.ds(pl.multiple_of((1 - core) * width, width), width), :] = other_half[i, 0:width, :]
            data[at, 2 * width : 2 * width + halves * local, :] = mine_half[i, width : width + halves * local, :]

    pps, qqs = [], []
    for s in range(slabs):
        both = data[s, 0:width, :]
        with_p = times(both, turned(both[:orbits], 3), 1)
        with_q = times(both, turned(both[orbits:], 3), 1)
        pps.append(with_p[:orbits])
        qqs.append(with_q[orbits:])
        if s > 0:
            up1[s - 1] = -with_q[:orbits]
            dn1[s - 1] = -with_p[orbits:]
    largest = None
    for s in range(slabs):
        base = qqs[s]
        if s + 1 < slabs:
            base = base + pps[s + 1]
        if s == 0:
            base = base + pps[0]
        for e in range(mine):
            row = 2 * width + ((e // share) ^ half) * local + first + e % share
            settings = data[s, pl.ds(row, 1), :]
            m = spot[s] * mine + e
            gains[m] = settings
            block = base + jnp.where(diag_lane, settings, 0.0)
            mat[m] = block
            rhs[m] = data[s, width : 2 * width, :]
            sums = jnp.sum(jnp.abs(block), axis=0, keepdims=True)
            largest = sums if largest is None else jnp.maximum(largest, sums)
    top = 1.01 * jnp.max(largest + half_roll(largest))
    copy_out(3, 0, slabs - 1)
    copy_out(4, 0, slabs - 1)

    def held(key):
        basic, place = places[key]
        return (up1, dn1, place) if basic else (up2, dn2, place)

    low = lane < orbits

    def real_rows(z):
        return jnp.concatenate([jnp.where(low, z, -z), half_roll(z)], axis=0)

    def packed(t, right):
        top, bottom = t[:orbits], t[orbits:]
        return jnp.where(low, half_roll(top), bottom) if right else jnp.where(low, top, half_roll(bottom))

    def around(depth, node, left, right, e):
        to_left = to_right = jnp.zeros((orbits, width), F32)
        inward = []
        if left is not None:
            ups, downs, place = held((depth, left, node, e))
            to_left = downs[place]
            inward.append(real_rows(ups[place]))
        if right is not None:
            ups, downs, place = held((depth, node, right, e))
            to_right = ups[place]
            inward.append(real_rows(downs[place]))
        outward = jnp.concatenate(
            [jnp.where(low, to_left, half_roll(to_right)), jnp.where(low, half_roll(to_left), to_right)], axis=0
        )
        return outward, inward[0] if len(inward) == 1 else jnp.concatenate(inward, axis=0)

    def settle(depth, node, left, right, e, step, inward):
        m = spot[node] * mine + e
        links_step, rhs_step = step[:, :width], step[:, width:]
        sol[m] = rhs_step
        change = times(inward, split(step, 3))
        if left is not None:
            w1[m] = packed(links_step, False)
            ml = spot[left] * mine + e
            mat[ml] = mat[ml] - packed(change[:width, :width], False)
            rhs[ml] = rhs[ml] - change[:width, width:]
        if right is not None:
            w2[m] = packed(links_step, True)
            mr = spot[right] * mine + e
            mat[mr] = mat[mr] - packed(change[-width:, :width], True)
            rhs[mr] = rhs[mr] - change[-width:, width:]
        if left is not None and right is not None:
            ups, downs, place = held((depth + 1, left, right, e))
            ups[place] = -packed(change[:width, :width], True)
            downs[place] = -packed(change[width:, :width], False)

    for depth, level in enumerate(levels):
        invert_batch(mat, inv, near, spot[level[0][0]] * mine, len(level) * mine, top)
        for node, left, right in level:
            if depth == 0:
                outward, inward = around(depth, node, left, right, 0)
                right_parts = split(jnp.concatenate([outward, rhs[spot[node] * mine]], axis=1), 3)
                inverses = [real_rows(inv[spot[node] * mine + e]) for e in range(mine)]
                step = times(jnp.concatenate(inverses, axis=0), right_parts)
                for e in range(mine):
                    settle(depth, node, left, right, e, step[e * width : (e + 1) * width], inward)
                continue
            for e in range(mine):
                m = spot[node] * mine + e
                outward, inward = around(depth, node, left, right, e)
                step = times(real_rows(inv[m]), split(jnp.concatenate([outward, rhs[m]], axis=1), 3))
                settle(depth, node, left, right, e, step, inward)
        span = [spot[node] * mine for node, _, _ in level]
        for which in range(3):
            copy_out(which, span[0], span[-1] + mine)
        made = [places[(depth + 1, l, r, e)][1] for _, l, r in level if l is not None and r is not None for e in range(mine)]
        if made:
            copy_out(5, made[0], made[-1] + 1)
            copy_out(6, made[0], made[-1] + 1)
    invert_batch(mat, inv, near, spot[root] * mine, mine, top)
    for e in range(mine):
        m = spot[root] * mine + e
        sol[m] = tall(times(inv[m], turned(wide(rhs[m]), 3)))
    copy_out(0, spot[root] * mine, (spot[root] + 1) * mine)

    def finished(nodes):
        copy_out(7, spot[nodes[0]] * mine, (spot[nodes[-1]] + 1) * mine)
        for s in nodes:
            for e in range(mine):
                xr, xi = orbitals_of(sol, spot[s] * mine + e, half, halves, orbits)
                power = xr * xr + xi * xi
                for j in range(lines):
                    power_ref[s // per, j, e, s % per, :, :] = power[j * orb_per : (j + 1) * orb_per, :]

    finished([root])
    climb(levels, spot, mine, w1, w2, sol, finished)
    for copy in copies:
        copy.wait()


def lesser_kernel(plan, where_ref, gains, *refs):
    (slabs, mine, orbits, groups, halves, lines, per, orb_per) = plan
    stores, out_ref = refs[:8], refs[8]
    inv, w1, w2, up1, dn1, up2, dn2, ret, rhs, sol, sems = refs[9:]
    held = (inv, w1, w2, up1, dn1, up2, dn2, ret)
    half = where_ref[3]
    width = 2 * orbits
    levels, root = elimination_levels(slabs)
    spot = slots(levels, root)
    places, _ = link_places(slabs, mine, levels)
    fetches = {}

    def fetch(which, depth, low_place, high_place):
        part = pl.ds(low_place, high_place - low_place)
        copy = pltpu.make_async_copy(stores[which].at[part], held[which].at[part], sems.at[len(fetches)])
        copy.start()
        fetches[(which, depth)] = copy

    spans = []
    for level in levels:
        span = [spot[node] * mine for node, _, _ in level]
        spans.append((span[0], span[-1] + mine))
    spans.append((spot[root] * mine, (spot[root] + 1) * mine))
    for depth, span in enumerate(spans):
        fetch(7, depth, *span)
        fetch(0, depth, *span)
        if depth == 0:
            fetch(3, 0, 0, slabs - 1)
            fetch(4, 0, 0, slabs - 1)
        elif depth < len(levels):
            level = levels[depth - 1]
            made = [places[(depth, l, r, e)][1] for _, l, r in level if l is not None and r is not None for e in range(mine)]
            if made:
                fetch(5, depth, made[0], made[-1] + 1)
                fetch(6, depth, made[0], made[-1] + 1)
    for depth in range(len(levels) - 1, -1, -1):
        fetch(1, depth, *spans[depth])
        fetch(2, depth, *spans[depth])
    for depth in range(len(spans)):
        fetches[(7, depth)].wait()
    lane = lax.broadcasted_iota(jnp.int32, (orbits, width), 1)
    sub = lax.broadcasted_iota(jnp.int32, (orbits, width), 0)
    gain_lane = lane == sub + orbits
    for m in range(slabs * mine):
        gain = jnp.sum(jnp.where(gain_lane, gains[m], 0.0), axis=1, keepdims=True)
        rhs[m] = wide(ret[m]) * gain
    for depth, level in enumerate(levels):
        for which in (0, 3, 4, 5, 6):
            if (which, depth) in fetches:
                fetches[(which, depth)].wait()

        def work(energies, depth=depth, level=level):
            items = [(node, left, right, e) for node, left, right in level for e in energies]
            steps = [times(inv[spot[node] * mine + e], turned(rhs[spot[node] * mine + e], 3)) for node, _, _, e in items]
            changes = []
            for (node, left, right, e), step in zip(items, steps):
                sides = []
                if left is not None:
                    basic, place = places[(depth, left, node, 0)]
                    sides.append(up1[place] if basic else up2[place + e])
                if right is not None:
                    basic, place = places[(depth, node, right, 0)]
                    sides.append(dn1[place] if basic else dn2[place + e])
                sides = sides[0] if len(sides) == 1 else jnp.concatenate(sides, axis=0)
                changes.append(times(sides, turned(step, 3)))
            for (node, left, right, e), step, change in zip(items, steps, changes):
                sol[spot[node] * mine + e] = tall(step)
                if left is not None:
                    ml = spot[left] * mine + e
                    rhs[ml] = rhs[ml] - change[:orbits]
                if right is not None:
                    mr = spot[right] * mine + e
                    rhs[mr] = rhs[mr] - change[-orbits:]

        over_energies(mine, len(level) > 2, work)
    fetches[(0, len(levels))].wait()
    for e in range(mine):
        m = spot[root] * mine + e
        sol[m] = tall(times(inv[m], turned(rhs[m], 3)))
    for depth in range(len(levels)):
        fetches[(1, depth)].wait()
        fetches[(2, depth)].wait()
    climb(levels, spot, mine, w1, w2, sol, lambda nodes: None)
    for s in range(slabs):
        for e in range(mine):
            m = spot[s] * mine + e
            xr, xi = orbitals_of(ret, m, half, halves, orbits)
            yr, yi = orbitals_of(sol, m, half, halves, orbits)
            re = xr * yr + xi * yi
            im = xr * yi - xi * yr
            for j in range(lines):
                rows = slice(j * orb_per, (j + 1) * orb_per)
                out_ref[s // per, j, 0, e, s % per, :, :] = re[rows, :]
                out_ref[s // per, j, 1, e, s % per, :, :] = im[rows, :]


def pack_kernel(where_ref, p_ref, q_ref, src_ref, *refs):
    settings, (factors_ref, parcel_ref) = refs[:-2], refs[-2:]
    per, _, orbits, _ = p_ref.shape
    width = 2 * orbits
    local = settings[0].shape[1]
    core = where_ref[2]
    for i in range(per):
        factors_ref[i, 0:orbits, :] = jnp.concatenate([p_ref[i, 0], p_ref[i, 1]], axis=1)
        factors_ref[i, orbits:width, :] = jnp.concatenate([q_ref[i, 0], q_ref[i, 1]], axis=1)
        for h, setting in enumerate(settings):
            parcel_ref[i, width + h * local : width + (h + 1) * local, :] = setting[i]

    @pl.when(core == 0)
    def _():
        parcel_ref[:, 0:width, :] = factors_ref[...]

    @pl.when(core != 0)
    def _():
        for i in range(per):
            parcel_ref[i, 0:orbits, :] = src_ref[i, 0]
            parcel_ref[i, orbits:width, :] = src_ref[i, 1]


def pack(where, link_p, link_q, sources, settings):
    per, _, orbits, _ = link_p.shape
    width = 2 * orbits
    rows = width + len(settings) * settings[0].shape[1]
    return pl.pallas_call(
        pack_kernel,
        out_shape=[
            jax.ShapeDtypeStruct((per, width, width), F32),
            jax.ShapeDtypeStruct((per, rows, sources.shape[-1]), F32),
        ],
        in_specs=[pl.BlockSpec(memory_space=pltpu.SMEM)] + vmem_specs(3 + len(settings)),
        out_specs=vmem_specs(2),
        compiler_params=pltpu.CompilerParams(vmem_limit_bytes=VMEM_LIMIT),
        name="pack_parcel",
    )(where, link_p, link_q, sources, *settings)


def vmem_specs(count):
    return [pl.BlockSpec(memory_space=pltpu.VMEM)] * count


def solve_retarded(where, pieces, plan, columns):
    (slabs, mine, orbits, groups, halves, lines, per, orb_per) = plan
    width = 2 * orbits
    nodes = slabs * mine
    levels, _ = elimination_levels(slabs)
    _, fills = link_places(slabs, mine, levels)
    kept = [
        (nodes, orbits, width),
        (nodes, orbits, width),
        (nodes, orbits, width),
        (slabs - 1, orbits, width),
        (slabs - 1, orbits, width),
        (fills, orbits, width),
        (fills, orbits, width),
        (nodes, width, columns),
    ]
    shapes = [(groups, lines, mine, per, orb_per, columns), (nodes, 1, width)] + kept
    return pl.pallas_call(
        functools.partial(retarded_kernel, plan),
        out_shape=[jax.ShapeDtypeStruct(shape, F32) for shape in shapes],
        in_specs=[pl.BlockSpec(memory_space=pltpu.SMEM)] + vmem_specs(len(pieces)),
        out_specs=vmem_specs(2) + [pl.BlockSpec(memory_space=pl.ANY)] * len(kept),
        scratch_shapes=[pltpu.VMEM(shape, F32) for shape in kept]
        + [
            pltpu.VMEM((slabs, 2 * width + halves * pieces[2].shape[1], columns), F32),
            pltpu.VMEM((nodes, orbits, width), F32),
            pltpu.VMEM((nodes, width, columns), F32),
            pltpu.VMEM((nodes, orbits, width), F32),
            pltpu.SemaphoreType.DMA((6 * len(levels) + 4,)),
        ],
        compiler_params=pltpu.CompilerParams(vmem_limit_bytes=VMEM_LIMIT),
        name="solve_retarded",
    )(where, *pieces)


def solve_lesser(where, stored, plan):
    (slabs, mine, orbits, groups, halves, lines, per, orb_per) = plan
    levels, _ = elimination_levels(slabs)
    gains, kept = stored[0], stored[1:]
    solved = kept[7].shape
    return pl.pallas_call(
        functools.partial(lesser_kernel, plan),
        out_shape=jax.ShapeDtypeStruct((groups, lines, 2, mine, per, orb_per, solved[-1]), F32),
        in_specs=[pl.BlockSpec(memory_space=pltpu.SMEM)]
        + vmem_specs(1)
        + [pl.BlockSpec(memory_space=pl.ANY)] * len(kept),
        out_specs=pl.BlockSpec(memory_space=pltpu.VMEM),
        scratch_shapes=[pltpu.VMEM(array.shape, F32) for array in kept]
        + [pltpu.VMEM((solved[0], solved[1] // 2, 2 * solved[2]), F32), pltpu.VMEM(solved, F32), pltpu.SemaphoreType.DMA((6 * len(levels) + 4,))],
        compiler_params=pltpu.CompilerParams(vmem_limit_bytes=VMEM_LIMIT),
        name="solve_lesser",
    )(where, gains, *kept)


def correlate_kernel(order, power_ref, got_ref, out_ref):
    count = len(order)
    window = 8
    scale = 1.0 / count
    for start in range(0, count, window):
        span = min(window, count - start)
        acc_re = [None] * span
        acc_im = [None] * span
        reach = count - start
        lead = {}
        for energy in range(reach):
            sender, place = order[energy]
            power = power_ref[sender, place, 0]
            for w in range(span):
                at = energy + start + w
                if at >= count:
                    continue
                if at not in lead:
                    s2, p2 = order[at]
                    lead[at] = (got_ref[s2, 0, p2, 0], got_ref[s2, 1, p2, 0])
                re, im = lead[at]
                acc_re[w] = re * power if acc_re[w] is None else acc_re[w] + re * power
                acc_im[w] = im * power if acc_im[w] is None else acc_im[w] + im * power
        for w in range(span):
            out_ref[0, start + w, 0] = acc_re[w] * scale
            out_ref[1, start + w, 0] = acc_im[w] * scale


def correlate(power, got, order):
    senders, kinds, mine, per, rows, columns = got.shape
    count = len(order)
    return pl.pallas_call(
        functools.partial(correlate_kernel, order),
        grid=(per,),
        out_shape=jax.ShapeDtypeStruct((2, count, per, rows, columns), F32),
        in_specs=[
            pl.BlockSpec((senders, mine, 1, rows, columns), lambda i: (0, 0, i, 0, 0)),
            pl.BlockSpec((senders, kinds, mine, 1, rows, columns), lambda i: (0, 0, 0, i, 0, 0)),
        ],
        out_specs=pl.BlockSpec((2, count, 1, rows, columns), lambda i: (0, 0, i, 0, 0)),
        compiler_params=pltpu.CompilerParams(vmem_limit_bytes=VMEM_LIMIT),
        name="correlate",
    )(power, got)


def per_device(link_p, link_q, shift, lesser_gain, sources):
    per, _, orbits, _ = link_p.shape
    columns = sources.shape[-1]
    local = shift.shape[0]
    groups = lax.axis_size("slab")
    halves = lax.axis_size("half")
    lines = lax.axis_size("line")
    slabs = per * groups
    share = max(1, local // groups)
    mine = halves * share
    owner = lax.axis_index("slab")
    half = lax.axis_index("half")
    core = lax.axis_index("line") & 1
    where = jnp.stack([owner * local // groups, owner, core, half]).astype(jnp.int32)
    settings = jnp.concatenate([jnp.swapaxes(shift, 0, 1), jnp.swapaxes(lesser_gain, 0, 1)], axis=-1)
    swaps = [[(a, a ^ h) for a in range(halves)] for h in range(1, halves)]
    settings = [settings] + [lax.ppermute(settings, "half", swap) for swap in swaps]
    factors, parcel = pack(where, link_p, link_q, sources, settings)
    pieces = [factors, sources, *settings]
    fetched = [lax.ppermute(parcel, "slab", [(g, g ^ k) for g in range(groups)]) for k in range(1, groups)]
    siblings = [(j, j ^ 1) for j in range(lines)]
    for piece in fetched:
        pieces.append(piece)
        pieces.append(lax.ppermute(piece, "line", siblings))
    plan = (slabs, mine, orbits, groups, halves, lines, per, orbits // (halves * lines))
    power, *stored = solve_retarded(where, pieces, plan, columns)

    def spread(array):
        array = array.reshape((groups * lines,) + array.shape[2:])
        return lax.all_to_all(array, ("slab", "line"), split_axis=0, concat_axis=0, tiled=True)

    power = spread(power)
    got = spread(solve_lesser(where, stored, plan))
    order = []
    for energy in range(halves * lines * local):
        group, row = energy // local, energy % local
        if local >= groups:
            holder, place = row // share, row % share
        else:
            holder, place = -(-row * groups // local), 0
        order.append((holder * lines + group % lines, (group // lines) * share + place))
    return correlate(power, got, tuple(order))


def solution(mesh):
    slab_size, energy_size = mesh.devices.shape
    halves = HALVES if energy_size % (2 * HALVES) == 0 else 1
    split = jax.sharding.Mesh(
        mesh.devices.reshape(slab_size, halves, energy_size // halves), ("slab", "half", "line")
    )
    placed = (
        P("slab", None, None, None),
        P("slab", None, None, None),
        P(("half", "line"), "slab", None),
        P(("half", "line"), "slab", None),
        P("slab", None, None, None),
    )
    return jax.shard_map(
        per_device,
        mesh=split,
        in_specs=placed,
        out_specs=P(None, None, "slab", ("half", "line"), None),
        check_vma=False,
    )
```

profile of v0, /device:TPU:0, one launch (start us, length us, event | category | flops | bytes accessed | tf_op | source)
XLA Modules:
  0.0 119.5 jit_solution(9166834520938810119)
XLA Ops:
  0.0 0.8 pad_maximum_fusion.refs_0_.refs_2_
  0.8 4.0 %collective-permute-start = (f32[3,8,128]{2,1,0:T(8,128)S(1)}, f32[3,8,128]{2,1,0:T(8,128)S(1)}, u32[]{:S(2)}, u32[]{:S(2)}) collective-permute-start(f32[3,8,128]{2,1,0:T(8,128)S(1)} %pad_maximum_fusion.refs_0_.refs_2_), channel_id=1, source_target_pairs={{0,4},{4,0},{1,5},{5,1},{2,6},{6,2},{3,7},{7,3},{8,12},{12,8},{9,1... | collective-permute-start | bytes 36872 | tf_op jit(solution)/shard_map/ppermute | solution.py:652
  4.8 0.6 pad_add_fusion.where_ref
  5.4 1.1 collective-permute-done.refs_1_.refs_3_
  6.5 0.0 copy-done.7
  6.5 0.6 copy-done.8
  7.1 2.0 %pack_parcel.1 = (f32[3,128,128]{2,1,0:T(8,128)}, f32[3,144,128]{2,1,0:T(8,128)}) custom-call(s32[4]{0:T(128)} %pad_add_fusion.where_ref, f32[3,2,64,64]{3,2,1,0:T(8,128)} %p_ref.1, f32[3,2,64,64]{3,2,1,0:T(8,128)} %q_ref.1, f32[3,2,64,128]{3,2,1,0:T(8,128)} %refs_1_.1, f32[3,8,128]{2,1,0:T(8,128)} %copy-done.7, f32[3,8,128]{2,1,0:T(8,128)} %copy-done.8), custom_call_target="tpu_custom_call" | custom-call | tf_op jit(solution)/shard_map/pack_parcel/pallas_call | solution.py:520
  9.1 2.8 %collective-permute-start.5 = (f32[3,144,128]{2,1,0:T(8,128)}, f32[3,144,128]{2,1,0:T(8,128)S(1)}, u32[]{:S(2)}, u32[]{:S(2)}) collective-permute-start(f32[3,144,128]{2,1,0:T(8,128)} %get-tuple-element.18), channel_id=1, source_target_pairs={{0,24},{8,16},{16,8},{24,0},{1,25},{9,17},{17,9},{25,1},{2,26},{10... | collective-permute-start | bytes 663560 | tf_op jit(solution)/shard_map/ppermute | solution.py:655
  11.9 0.5 collective-permute-start.3
  12.4 0.2 collective-permute-start.1
  12.6 6.0 %collective-permute-done.5.refs_8_ = f32[3,144,128]{2,1,0:T(8,128)S(1)} collective-permute-done((f32[3,144,128]{2,1,0:T(8,128)}, f32[3,144,128]{2,1,0:T(8,128)S(1)}, u32[]{:S(2)}, u32[]{:S(2)}) %collective-permute-start.5) | collective-permute-done | bytes 221216 | tf_op jit(solution)/shard_map/ppermute | solution.py:655
  18.6 0.0 collective-permute-start.6
  18.6 2.7 %collective-permute-done.3.refs_6_ = f32[3,144,128]{2,1,0:T(8,128)S(1)} collective-permute-done((f32[3,144,128]{2,1,0:T(8,128)}, f32[3,144,128]{2,1,0:T(8,128)S(1)}, u32[]{:S(2)}, u32[]{:S(2)}) %collective-permute-start.3) | collective-permute-done | bytes 221216 | tf_op jit(solution)/shard_map/ppermute | solution.py:655
  21.3 0.0 collective-permute-start.4
  21.3 0.1 collective-permute-done.1.refs_4_
  21.4 0.4 collective-permute-start.2
  21.8 0.0 collective-permute-done.6.refs_9_
  21.8 1.0 collective-permute-done.4.refs_7_
  22.8 0.3 collective-permute-done.2.refs_5_
  23.1 0.0 copy-done.1
  23.1 0.0 copy-done.2
  23.1 0.0 copy-done.3
  23.1 0.0 copy-done.4
  23.1 0.3 copy-done.5
  23.5 0.3 copy-done.6
  23.8 41.6 %solve_retarded.1 = (f32[4,4,4,3,8,128]{5,4,3,2,1,0:T(8,128)}, f32[48,1,128]{2,1,0:T(1,128)}, f32[48,64,128]{2,1,0:T(8,128)}, f32[48,64,128]{2,1,0:T(8,128)}, f3...) custom-call(s32[4]{0:T(128)} %pad_add_fusion.where_ref, ...), custom_call_target="tpu_custom_call" | custom-call | tf_op jit(solution)/shard_map/solve_retarded/pallas_call | solution.py:554
  65.3 4.2 %all-to-all-start = ((f32[16,4,3,8,128]{4,3,2,1,0:T(8,128)}), f32[16,4,3,8,128]{4,3,2,1,0:T(8,128)S(1)}, u32[]{:S(2)}, u32[]{:S(2)}) async-start(f32[16,4,3,8,128]{4,3,2,1,0:T(8,128)} %bitcast.9), calls=%async_computation | async-start | bytes 1572864 | tf_op jit(solution)/shard_map/all_to_all | solution.py:665
  69.6 15.8 %solve_lesser.1 = f32[4,4,2,4,3,8,128]{6,5,4,3,2,1,0:T(8,128)} custom-call(s32[4]{0:T(128)} %pad_add_fusion.where_ref, f32[48,1,128]{2,1,0:T(1,128)} %get-tuple-element.20.gains, f32[48,64,128]{2,1,0:T(8,128)} %get-tuple-element.21.refs_0_, f32[48,64,128]{2,1,0:T(8,128)} %get-tuple-element.22.refs_1_, f32[48,64,128]{2,1,0:T(8,128)} %get-tuple-element.23.refs_2_, ...), custom_call_target="tpu_custom_call" | custom-call | tf_op jit(solution)/shard_map/solve_lesser/pallas_call | solution.py:577
  85.3 0.0 all-to-all-done.power_ref
  85.4 0.0 copy-start
  85.4 27.0 %all_to_all.10.got_ref = f32[16,2,4,3,8,128]{5,4,3,2,1,0:T(8,128)} all-to-all(f32[16,2,4,3,8,128]{5,4,3,2,1,0:T(8,128)} %bitcast.8), channel_id=1, replica_groups=mesh['slab'=4,'half'=2,'line'=4] {'slab','line'}, dimensions={0} | all-to-all | bytes 3145728 | tf_op jit(solution)/shard_map/all_to_all | solution.py:665
  112.4 7.1 %correlate.1 = f32[2,64,3,8,128]{4,3,2,1,0:T(8,128)} custom-call(f32[16,4,3,8,128]{4,3,2,1,0:T(8,128)} %copy-done, f32[16,2,4,3,8,128]{5,4,3,2,1,0:T(8,128)} %all_to_all.10.got_ref), custom_call_target="tpu_custom_call" | custom-call | tf_op jit(solution)/shard_map/correlate/pallas_call | solution.py:622
  (9 shorter events, 0.0 us)
Async XLA Ops:
  0.8 5.7 %copy-start.7 = (f32[3,8,128]{2,1,0:T(8,128)}, f32[3,8,128]{2,1,0:T(8,128)S(1)}, u32[]{:S(2)}) copy-start(f32[3,8,128]{2,1,0:T(8,128)S(1)} %pad_maximum_fusion.refs_0_.refs_2_) | copy-start | bytes 36868
  0.8 5.7 %collective-permute-start = (f32[3,8,128]{2,1,0:T(8,128)S(1)}, f32[3,8,128]{2,1,0:T(8,128)S(1)}, u32[]{:S(2)}, u32[]{:S(2)}) collective-permute-start(f32[3,8,128]{2,1,0:T(8,128)S(1)} %pad_maximum_fusion.refs_0_.refs_2_), channel_id=1, source_target_pairs={{0,4},{4,0},{1,5},{5,1},{2,6},{6,2},{3,7},{7,3},{8,12},{12,8},{9,1... | collective-permute-start | bytes 36872 | tf_op jit(solution)/shard_map/ppermute | solution.py:652
  6.5 0.6 copy-start.8
  9.1 9.5 %collective-permute-start.5 = (f32[3,144,128]{2,1,0:T(8,128)}, f32[3,144,128]{2,1,0:T(8,128)S(1)}, u32[]{:S(2)}, u32[]{:S(2)}) collective-permute-start(f32[3,144,128]{2,1,0:T(8,128)} %get-tuple-element.18), channel_id=1, source_target_pairs={{0,24},{8,16},{16,8},{24,0},{1,25},{9,17},{17,9},{25,1},{2,26},{10... | collective-permute-start | bytes 663560 | tf_op jit(solution)/shard_map/ppermute | solution.py:655
  11.9 9.4 %collective-permute-start.3 = (f32[3,144,128]{2,1,0:T(8,128)}, f32[3,144,128]{2,1,0:T(8,128)S(1)}, u32[]{:S(2)}, u32[]{:S(2)}) collective-permute-start(f32[3,144,128]{2,1,0:T(8,128)} %get-tuple-element.18), channel_id=1, source_target_pairs={{0,16},{8,24},{16,0},{24,8},{1,17},{9,25},{17,1},{25,9},{2,18},{10... | collective-permute-start | bytes 663560 | tf_op jit(solution)/shard_map/ppermute | solution.py:655
  12.4 9.0 %collective-permute-start.1 = (f32[3,144,128]{2,1,0:T(8,128)}, f32[3,144,128]{2,1,0:T(8,128)S(1)}, u32[]{:S(2)}, u32[]{:S(2)}) collective-permute-start(f32[3,144,128]{2,1,0:T(8,128)} %get-tuple-element.18), channel_id=1, source_target_pairs={{0,8},{8,0},{16,24},{24,16},{1,9},{9,1},{17,25},{25,17},{2,10},{10... | collective-permute-start | bytes 663560 | tf_op jit(solution)/shard_map/ppermute | solution.py:655
  18.6 4.5 %copy-start.1 = (f32[3,144,128]{2,1,0:T(8,128)}, f32[3,144,128]{2,1,0:T(8,128)S(1)}, u32[]{:S(2)}) copy-start(f32[3,144,128]{2,1,0:T(8,128)S(1)} %collective-permute-done.5.refs_8_) | copy-start | bytes 663556
  18.6 3.2 %collective-permute-start.6 = (f32[3,144,128]{2,1,0:T(8,128)S(1)}, f32[3,144,128]{2,1,0:T(8,128)S(1)}, u32[]{:S(2)}, u32[]{:S(2)}) collective-permute-start(f32[3,144,128]{2,1,0:T(8,128)S(1)} %collective-permute-done.5.refs_8_), channel_id=1, source_target_pairs={{0,1},{1,0},{2,3},{3,2},{4,5},{5,4},{6,7},{7,6},{8,9},{9,8},{10,11... | collective-permute-start | bytes 663560 | tf_op jit(solution)/shard_map/ppermute | solution.py:659
  21.3 1.8 %copy-start.2 = (f32[3,144,128]{2,1,0:T(8,128)}, f32[3,144,128]{2,1,0:T(8,128)S(1)}, u32[]{:S(2)}) copy-start(f32[3,144,128]{2,1,0:T(8,128)S(1)} %collective-permute-done.3.refs_6_) | copy-start | bytes 663556
  21.3 1.5 %collective-permute-start.4 = (f32[3,144,128]{2,1,0:T(8,128)S(1)}, f32[3,144,128]{2,1,0:T(8,128)S(1)}, u32[]{:S(2)}, u32[]{:S(2)}) collective-permute-start(f32[3,144,128]{2,1,0:T(8,128)S(1)} %collective-permute-done.3.refs_6_), channel_id=1, source_target_pairs={{0,1},{1,0},{2,3},{3,2},{4,5},{5,4},{6,7},{7,6},{8,9},{9,8},{10,11... | collective-permute-start | bytes 663560 | tf_op jit(solution)/shard_map/ppermute | solution.py:659
  21.4 1.7 %copy-start.3 = (f32[3,144,128]{2,1,0:T(8,128)}, f32[3,144,128]{2,1,0:T(8,128)S(1)}, u32[]{:S(2)}) copy-start(f32[3,144,128]{2,1,0:T(8,128)S(1)} %collective-permute-done.1.refs_4_) | copy-start | bytes 663556
  21.4 1.6 %collective-permute-start.2 = (f32[3,144,128]{2,1,0:T(8,128)S(1)}, f32[3,144,128]{2,1,0:T(8,128)S(1)}, u32[]{:S(2)}, u32[]{:S(2)}) collective-permute-start(f32[3,144,128]{2,1,0:T(8,128)S(1)} %collective-permute-done.1.refs_4_), channel_id=1, source_target_pairs={{0,1},{1,0},{2,3},{3,2},{4,5},{5,4},{6,7},{7,6},{8,9},{9,8},{10,11... | collective-permute-start | bytes 663560 | tf_op jit(solution)/shard_map/ppermute | solution.py:659
  21.8 1.3 %copy-start.4 = (f32[3,144,128]{2,1,0:T(8,128)}, f32[3,144,128]{2,1,0:T(8,128)S(1)}, u32[]{:S(2)}) copy-start(f32[3,144,128]{2,1,0:T(8,128)S(1)} %collective-permute-done.6.refs_9_) | copy-start | bytes 663556
  22.8 0.7 copy-start.5
  23.1 0.7 copy-start.6
  65.3 20.0 %all-to-all-start = ((f32[16,4,3,8,128]{4,3,2,1,0:T(8,128)}), f32[16,4,3,8,128]{4,3,2,1,0:T(8,128)S(1)}, u32[]{:S(2)}, u32[]{:S(2)}) async-start(f32[16,4,3,8,128]{4,3,2,1,0:T(8,128)} %bitcast.9), calls=%async_computation | async-start | bytes 1572864 | tf_op jit(solution)/shard_map/all_to_all | solution.py:665
  85.4 27.0 %copy-start = (f32[16,4,3,8,128]{4,3,2,1,0:T(8,128)}, f32[16,4,3,8,128]{4,3,2,1,0:T(8,128)S(1)}, u32[]{:S(2)}) copy-start(f32[16,4,3,8,128]{4,3,2,1,0:T(8,128)S(1)} %all-to-all-done.power_ref) | copy-start | bytes 2359300
where the time goes:
time: 120 us; the launch traced here: 119 us
  Pallas kernels  66.5 us (55%)
  blocking collectives  27 us (22%)
  starting transfers between devices  12.1 us (10%)
  waiting for transfers between devices  11.2 us (9%)
  other arithmetic  1.39 us (1%)
  local copies, waits for them, and re-layouts  1.3 us (1%)
    pallas_call x1, Pallas kernels, solve_retarded(): pl.pallas_call(functools.partial(retarded_kernel, plan), out_shape=[jax.S...  41.6 us
    all_to_all x1, blocking collectives, spread(): lax.all_to_all(array, ('slab', 'line'), split_axis=0, concat_axis=0, tile...  27 us
    pallas_call x1, Pallas kernels, solve_lesser(): pl.pallas_call(functools.partial(lesser_kernel, plan), out_shape=jax.Shap...  15.8 us
    ppermute x3, waiting for transfers between devices, per_device(): lax.ppermute(parcel, 'slab', [(g, g ^ k) for g in range(groups)])  8.8 us
    pallas_call x1, Pallas kernels, correlate(): pl.pallas_call(functools.partial(correlate_kernel, order), grid=(per,), o...  7.11 us
    all_to_all x1, starting transfers between devices, spread(): lax.all_to_all(array, ('slab', 'line'), split_axis=0, concat_axis=0, tile...  4.21 us
    ppermute x1, starting transfers between devices, per_device(): lax.ppermute(settings, 'half', swap)  4.05 us
    ppermute x3, starting transfers between devices, per_device(): lax.ppermute(parcel, 'slab', [(g, g ^ k) for g in range(groups)])  3.49 us
  transfers between devices with their start and end apart: 8, of which 6 were waited for; matrix products, arithmetic and copies ran while one was open for 0% of the time, Pallas kernels for 13%

commit v1 on v0

--- a/solution.py
+++ b/solution.py
@@ -13,7 +13,7 @@
 LEAST = 0.0095
 CLOSE = 1e-3
 STRIDE = 4
-GROUP = 12
+GROUP = 8
 HALVES = 2
 
 
@@ -102,21 +102,21 @@
         work(list(range(mine)))
 
 
-def invert_batch(mat_ref, inv_ref, near_ref, first, number, top):
+def invert_batch(mat_ref, inv_ref, first, number, top):
     size = next(size for size in range(min(number, GROUP), 0, -1) if number % size == 0)
     if size == number:
-        invert_group(mat_ref, inv_ref, near_ref, range(first, first + number), top)
+        invert_group(mat_ref, inv_ref, range(first, first + number), top)
     else:
 
         def group(place, unused):
             begin = first + place * size
-            invert_group(mat_ref, inv_ref, near_ref, [begin + n for n in range(size)], top)
+            invert_group(mat_ref, inv_ref, [begin + n for n in range(size)], top)
             return 0
 
         lax.fori_loop(0, number // size, group, 0)
 
 
-def invert_group(mat_ref, inv_ref, near_ref, members, top):
+def invert_group(mat_ref, inv_ref, members, top):
     shape = mat_ref.shape[1:]
     count = shape[0]
     lane = lax.broadcasted_iota(jnp.int32, shape, 1)
@@ -129,41 +129,34 @@
         gain = 2.0 / (2.0 - squared)
         return gain, 0.5 * squared * gain
 
-    def pair_step(unused, reach):
-        gain, after = factor_of(reach)
-        ts = [near_ref[m] for m in members]
-        both = [jnp.concatenate([inv_ref[m], t], axis=0) for m, t in zip(members, ts)]
-        pairs = [times(x, turned((2.0 * eye - t) * gain, 2)) for x, t in zip(both, ts)]
-        for m, pair in zip(members, pairs):
-            inv_ref[m] = pair[:count]
-            near_ref[m] = pair[count:]
-        return after
-
-    def cycle(state):
-        number, reach = state
-        reach = lax.fori_loop(0, number, pair_step, reach)
-        gain, after = factor_of(reach)
-        xs = [times(inv_ref[m], turned((2.0 * eye - near_ref[m]) * gain, 2)) for m in members]
+    def steps(xs, ts, reach, number):
+        for step in range(number):
+            gain, reach = factor_of(reach)
+            bases = [(2.0 * eye - t) * gain for t in ts]
+            if step + 1 < number:
+                pairs = [times(jnp.concatenate([x, t], axis=0), turned(base, 2)) for x, t, base in zip(xs, ts, bases)]
+                xs = [pair[:count] for pair in pairs]
+                ts = [pair[count:] for pair in pairs]
+            else:
+                xs = [times(x, turned(base, 2)) for x, base in zip(xs, bases)]
         for m, x in zip(members, xs):
             inv_ref[m] = x
-
-        @pl.when(after > CLOSE)
-        def _():
-            ts = [times(mat_ref[m], turned(inv_ref[m], 2)) for m in members]
-            for m, t in zip(members, ts):
-                near_ref[m] = t
-
-        return jnp.int32(STRIDE - 1), after
+        return reach
 
     start = 2.0 / total
     gain, reach = factor_of((top - LEAST) / total)
     ts = [mat_ref[m] * start for m in members]
     bases = [(2.0 * eye - t) * gain for t in ts]
-    products = [times(t, turned(base, 2)) for t, base in zip(ts, bases)]
-    for m, base, product in zip(members, bases, products):
-        inv_ref[m] = base * start
-        near_ref[m] = product
-    lax.while_loop(lambda state: state[1] > CLOSE, cycle, (jnp.int32(STRIDE - 2), reach))
+    xs = [base * start for base in bases]
+    ts = [times(t, turned(base, 2)) for t, base in zip(ts, bases)]
+    reach = steps(xs, ts, reach, STRIDE - 1)
+
+    def cycle(reach):
+        xs = [inv_ref[m] for m in members]
+        ts = [times(mat_ref[m], turned(x, 2)) for m, x in zip(members, xs)]
+        return steps(xs, ts, reach, STRIDE)
+
+    lax.while_loop(lambda reach: reach > CLOSE, cycle, reach)
     xs = [inv_ref[m] for m in members]
     rests = [eye - times(mat_ref[m], turned(x, 3)) for m, x in zip(members, xs)]
     for m, x, rest in zip(members, xs, rests):
@@ -227,14 +220,13 @@
 
 def retarded_kernel(plan, where_ref, *refs):
     (slabs, mine, orbits, groups, halves, lines, per, orb_per) = plan
-    factors_ref, src_ref = refs[:2]
-    own_settings = refs[2 : 2 + halves]
-    refs = refs[2 + halves :]
-    peers = refs[: 2 * (groups - 1)]
-    refs = refs[2 * (groups - 1) :]
-    local = own_settings[0].shape[1]
+    factors_ref, src_ref, settings_ref = refs[:3]
+    peers = refs[3 : 3 + 2 * (groups - 1)]
+    refs = refs[3 + 2 * (groups - 1) :]
+    others, refs = refs[: halves - 1], refs[halves - 1 :]
+    local = settings_ref.shape[1]
     power_ref, gains, outs = refs[0], refs[1], refs[2:10]
-    inv, w1, w2, up1, dn1, up2, dn2, sol, data, mat, rhs, near, sems = refs[10:]
+    inv, w1, w2, up1, dn1, up2, dn2, sol, data, mat, rhs, hold, sems = refs[10:]
     stores = (inv, w1, w2, up1, dn1, up2, dn2, sol)
     copies = []
 
@@ -260,15 +252,19 @@
         data[at, 0:width, :] = factors_ref[i]
         data[at, width : width + orbits, :] = src_ref[i, 0]
         data[at, width + orbits : 2 * width, :] = src_ref[i, 1]
-        for h in range(halves):
-            data[at, 2 * width + h * local : 2 * width + (h + 1) * local, :] = own_settings[h][i]
+        data[at, 2 * width : 2 * width + local, :] = settings_ref[i]
     for k in range(1, groups):
         mine_half, other_half = peers[2 * (k - 1)], peers[2 * (k - 1) + 1]
         for i in range(per):
             at = (owner ^ k) * per + i
             data[at, pl.ds(pl.multiple_of(core * width, width), width), :] = mine_half[i, 0:width, :]
             data[at, pl.ds(pl.multiple_of((1 - core) * width, width), width), :] = other_half[i, 0:width, :]
-            data[at, 2 * width : 2 * width + halves * local, :] = mine_half[i, width : width + halves * local, :]
+            data[at, 2 * width : 2 * width + local, :] = mine_half[i, width : width + local, :]
+    for h in range(1, halves):
+        for k in range(groups):
+            for i in range(per):
+                at = (owner ^ k) * per + i
+                data[at, 2 * width + h * local : 2 * width + (h + 1) * local, :] = others[h - 1][k * per + i]
 
     pps, qqs = [], []
     for s in range(slabs):
@@ -301,9 +297,9 @@
     copy_out(3, 0, slabs - 1)
     copy_out(4, 0, slabs - 1)
 
-    def held(key):
-        basic, place = places[key]
-        return (up1, dn1, place) if basic else (up2, dn2, place)
+    def held(depth, left, right, e):
+        basic, place = places[(depth, left, right, 0)]
+        return (up1, dn1, place) if basic else (up2, dn2, place + e)
 
     low = lane < orbits
 
@@ -318,11 +314,11 @@
         to_left = to_right = jnp.zeros((orbits, width), F32)
         inward = []
         if left is not None:
-            ups, downs, place = held((depth, left, node, e))
+            ups, downs, place = held(depth, left, node, e)
             to_left = downs[place]
             inward.append(real_rows(ups[place]))
         if right is not None:
-            ups, downs, place = held((depth, node, right, e))
+            ups, downs, place = held(depth, node, right, e)
             to_right = ups[place]
             inward.append(real_rows(downs[place]))
         outward = jnp.concatenate(
@@ -346,26 +342,37 @@
             mat[mr] = mat[mr] - packed(change[-width:, :width], True)
             rhs[mr] = rhs[mr] - change[-width:, width:]
         if left is not None and right is not None:
-            ups, downs, place = held((depth + 1, left, right, e))
+            ups, downs, place = held(depth + 1, left, right, e)
             ups[place] = -packed(change[:width, :width], True)
             downs[place] = -packed(change[width:, :width], False)
 
     for depth, level in enumerate(levels):
-        invert_batch(mat, inv, near, spot[level[0][0]] * mine, len(level) * mine, top)
-        for node, left, right in level:
-            if depth == 0:
-                outward, inward = around(depth, node, left, right, 0)
-                right_parts = split(jnp.concatenate([outward, rhs[spot[node] * mine]], axis=1), 3)
-                inverses = [real_rows(inv[spot[node] * mine + e]) for e in range(mine)]
+        invert_batch(mat, inv, spot[level[0][0]] * mine, len(level) * mine, top)
+        if depth == 0:
+            for node, left, right in level:
+                at = spot[node] * mine
+                outward, _ = around(depth, node, left, right, 0)
+                inverses = [real_rows(inv[at + e]) for e in range(mine)]
+                right_parts = split(jnp.concatenate([outward, rhs[at]], axis=1), 3)
                 step = times(jnp.concatenate(inverses, axis=0), right_parts)
                 for e in range(mine):
-                    settle(depth, node, left, right, e, step[e * width : (e + 1) * width], inward)
-                continue
-            for e in range(mine):
-                m = spot[node] * mine + e
-                outward, inward = around(depth, node, left, right, e)
-                step = times(real_rows(inv[m]), split(jnp.concatenate([outward, rhs[m]], axis=1), 3))
+                    hold[at + e] = step[e * width : (e + 1) * width]
+
+        def work(energies, depth=depth, level=level):
+            found = []
+            for node, left, right in level:
+                for e in energies:
+                    m = spot[node] * mine + e
+                    outward, inward = around(depth, node, left, right, e)
+                    if depth == 0:
+                        step = hold[m]
+                    else:
+                        step = times(real_rows(inv[m]), split(jnp.concatenate([outward, rhs[m]], axis=1), 3))
+                    found.append((node, left, right, e, step, inward))
+            for node, left, right, e, step, inward in found:
                 settle(depth, node, left, right, e, step, inward)
+
+        over_energies(mine, len(level) > 2, work)
         span = [spot[node] * mine for node, _, _ in level]
         for which in range(3):
             copy_out(which, span[0], span[-1] + mine)
@@ -373,7 +380,7 @@
         if made:
             copy_out(5, made[0], made[-1] + 1)
             copy_out(6, made[0], made[-1] + 1)
-    invert_batch(mat, inv, near, spot[root] * mine, mine, top)
+    invert_batch(mat, inv, spot[root] * mine, mine, top)
     for e in range(mine):
         m = spot[root] * mine + e
         sol[m] = tall(times(inv[m], turned(wide(rhs[m]), 3)))
@@ -468,7 +475,7 @@
                     mr = spot[right] * mine + e
                     rhs[mr] = rhs[mr] - change[-orbits:]
 
-        over_energies(mine, len(level) > 2, work)
+        over_energies(mine, len(level) > 1, work)
     fetches[(0, len(levels))].wait()
     for e in range(mine):
         m = spot[root] * mine + e
@@ -490,17 +497,17 @@
                 out_ref[s // per, j, 1, e, s % per, :, :] = im[rows, :]
 
 
-def pack_kernel(where_ref, p_ref, q_ref, src_ref, *refs):
-    settings, (factors_ref, parcel_ref) = refs[:-2], refs[-2:]
+def pack_kernel(where_ref, p_ref, q_ref, src_ref, shift_ref, gain_ref, factors_ref, settings_ref, parcel_ref):
     per, _, orbits, _ = p_ref.shape
     width = 2 * orbits
-    local = settings[0].shape[1]
+    local = shift_ref.shape[1]
     core = where_ref[2]
     for i in range(per):
+        settings = jnp.concatenate([shift_ref[i], gain_ref[i]], axis=1)
+        settings_ref[i] = settings
+        parcel_ref[i, width : width + local, :] = settings
         factors_ref[i, 0:orbits, :] = jnp.concatenate([p_ref[i, 0], p_ref[i, 1]], axis=1)
         factors_ref[i, orbits:width, :] = jnp.concatenate([q_ref[i, 0], q_ref[i, 1]], axis=1)
-        for h, setting in enumerate(settings):
-            parcel_ref[i, width + h * local : width + (h + 1) * local, :] = setting[i]
 
     @pl.when(core == 0)
     def _():
@@ -513,21 +520,19 @@
             parcel_ref[i, orbits:width, :] = src_ref[i, 1]
 
 
-def pack(where, link_p, link_q, sources, settings):
+def pack(where, link_p, link_q, sources, shift, lesser_gain):
     per, _, orbits, _ = link_p.shape
     width = 2 * orbits
-    rows = width + len(settings) * settings[0].shape[1]
+    local = shift.shape[1]
+    shapes = [(per, width, width), (per, local, width), (per, width + local, sources.shape[-1])]
     return pl.pallas_call(
         pack_kernel,
-        out_shape=[
-            jax.ShapeDtypeStruct((per, width, width), F32),
-            jax.ShapeDtypeStruct((per, rows, sources.shape[-1]), F32),
-        ],
-        in_specs=[pl.BlockSpec(memory_space=pltpu.SMEM)] + vmem_specs(3 + len(settings)),
-        out_specs=vmem_specs(2),
+        out_shape=[jax.ShapeDtypeStruct(shape, F32) for shape in shapes],
+        in_specs=[pl.BlockSpec(memory_space=pltpu.SMEM)] + vmem_specs(5),
+        out_specs=vmem_specs(3),
         compiler_params=pltpu.CompilerParams(vmem_limit_bytes=VMEM_LIMIT),
         name="pack_parcel",
-    )(where, link_p, link_q, sources, *settings)
+    )(where, link_p, link_q, sources, shift, lesser_gain)
 
 
 def vmem_specs(count):
@@ -561,7 +566,7 @@
             pltpu.VMEM((slabs, 2 * width + halves * pieces[2].shape[1], columns), F32),
             pltpu.VMEM((nodes, orbits, width), F32),
             pltpu.VMEM((nodes, width, columns), F32),
-            pltpu.VMEM((nodes, orbits, width), F32),
+            pltpu.VMEM((len(levels[0]) * mine, width, 2 * width), F32),
             pltpu.SemaphoreType.DMA((6 * len(levels) + 4,)),
         ],
         compiler_params=pltpu.CompilerParams(vmem_limit_bytes=VMEM_LIMIT),
@@ -647,16 +652,18 @@
     half = lax.axis_index("half")
     core = lax.axis_index("line") & 1
     where = jnp.stack([owner * local // groups, owner, core, half]).astype(jnp.int32)
-    settings = jnp.concatenate([jnp.swapaxes(shift, 0, 1), jnp.swapaxes(lesser_gain, 0, 1)], axis=-1)
-    swaps = [[(a, a ^ h) for a in range(halves)] for h in range(1, halves)]
-    settings = [settings] + [lax.ppermute(settings, "half", swap) for swap in swaps]
-    factors, parcel = pack(where, link_p, link_q, sources, settings)
-    pieces = [factors, sources, *settings]
+    factors, settings, parcel = pack(
+        where, link_p, link_q, sources, jnp.swapaxes(shift, 0, 1), jnp.swapaxes(lesser_gain, 0, 1)
+    )
+    pieces = [factors, sources, settings]
     fetched = [lax.ppermute(parcel, "slab", [(g, g ^ k) for g in range(groups)]) for k in range(1, groups)]
     siblings = [(j, j ^ 1) for j in range(lines)]
     for piece in fetched:
         pieces.append(piece)
         pieces.append(lax.ppermute(piece, "line", siblings))
+    known = jnp.concatenate([settings] + [piece[:, 2 * orbits :] for piece in fetched], axis=0)
+    for h in range(1, halves):
+        pieces.append(lax.ppermute(known, "half", [(a, a ^ h) for a in range(halves)]))
     plan = (slabs, mine, orbits, groups, halves, lines, per, orbits // (halves * lines))
     power, *stored = solve_retarded(where, pieces, plan, columns)
 

time: 120 us -> 118 us (0.983)
  Pallas kernels: 66.5 us -> 64.8 us
    pallas_call x1, Pallas kernels: 41.6 us -> 39.7 us  [solve_retarded(): pl.pallas_call(functools.partial(retarded_kernel, plan), out_shape=[jax.S...]
    ppermute x1, waiting for transfers between devices: 1.08 us -> 2.73 us  [per_device(): lax.ppermute(known, 'half', [(a, a ^ h) for a in range(halves)])]
    ppermute x3, waiting for transfers between devices: 1.27 us -> 0.01 us  [per_device(): pieces.append(lax.ppermute(piece, 'line', siblings))]
    ppermute x1, starting transfers between devices: 4.05 us -> 2.78 us  [per_device(): lax.ppermute(known, 'half', [(a, a ^ h) for a in range(halves)])]
  transfers between devices with their start and end apart: 8 -> 8, of which waited for: 6 -> 4; matrix products, arithmetic and copies ran while one was open for 0% -> 1% of each run, Pallas kernels for 13% -> 14%
where the time goes in v1:
time: 118 us
  Pallas kernels  64.8 us (55%)
  blocking collectives  27 us (23%)
  waiting for transfers between devices  12.3 us (10%)
  starting transfers between devices  11.3 us (10%)
  other arithmetic  1.36 us (1%)
    pallas_call x1, Pallas kernels, solve_retarded(): pl.pallas_call(functools.partial(retarded_kernel, plan), out_shape=[jax.S...  39.7 us
    all_to_all x1, blocking collectives, spread(): lax.all_to_all(array, ('slab', 'line'), split_axis=0, concat_axis=0, tile...  27 us
    pallas_call x1, Pallas kernels, solve_lesser(): pl.pallas_call(functools.partial(lesser_kernel, plan), out_shape=jax.Shap...  16 us
    ppermute x3, waiting for transfers between devices, per_device(): lax.ppermute(parcel, 'slab', [(g, g ^ k) for g in range(groups)])  9.55 us
    pallas_call x1, Pallas kernels, correlate(): pl.pallas_call(functools.partial(correlate_kernel, order), grid=(per,), o...  7.11 us
    ppermute x3, starting transfers between devices, per_device(): lax.ppermute(parcel, 'slab', [(g, g ^ k) for g in range(groups)])  4.46 us
    all_to_all x1, starting transfers between devices, spread(): lax.all_to_all(array, ('slab', 'line'), split_axis=0, concat_axis=0, tile...  3.81 us
    ppermute x1, starting transfers between devices, per_device(): lax.ppermute(known, 'half', [(a, a ^ h) for a in range(halves)])  2.78 us
  transfers between devices with their start and end apart: 8, of which 4 were waited for; matrix products, arithmetic and copies ran while one was open for 1% of the time, Pallas kernels for 14%

profile of v1, /device:TPU:0, one launch (start us, length us, event | category | flops | bytes accessed | tf_op | source)
XLA Modules:
  0.0 117.6 jit_solution(9739503900795486835)
XLA Ops:
  0.0 0.7 pad_add_fusion.where_ref
  0.7 2.0 %pack_parcel.1 = (f32[3,128,128]{2,1,0:T(8,128)}, f32[3,8,128]{2,1,0:T(8,128)}, f32[3,136,128]{2,1,0:T(8,128)}) custom-call(s32[4]{0:T(128)} %pad_add_fusion.where_ref, f32[3,2,64,64]{3,2,1,0:T(8,128)} %p_ref.1, f32[3,2,64,64]{3,2,1,0:T(8,128)} %q_ref.1, f32[3,2,64,128]{3,2,1,0:T(8,128)} %refs_1_.1, f32[3,8,64]{2,1,0:T(8,128)} %bitcast.10, f32[3,8,64]{2,1,0:T(8,128)} %bitcast.11), custom_call_target="tpu_custom_call" | custom-call | tf_op jit(solution)/shard_map/pack_parcel/pallas_call | solution.py:528
  2.7 3.9 %collective-permute-start.4 = (f32[3,136,128]{2,1,0:T(8,128)}, f32[3,136,128]{2,1,0:T(8,128)S(1)}, u32[]{:S(2)}, u32[]{:S(2)}) collective-permute-start(f32[3,136,128]{2,1,0:T(8,128)} %get-tuple-element.20), channel_id=1, source_target_pairs={{0,24},{8,16},{16,8},{24,0},{1,25},{9,17},{17,9},{25,1},{2,26},{10... | collective-permute-start | bytes 626696 | tf_op jit(solution)/shard_map/ppermute | solution.py:659
  6.6 0.5 collective-permute-start.2
  7.1 0.1 collective-permute-start
  7.1 5.7 %collective-permute-done.4.refs_7_ = f32[3,136,128]{2,1,0:T(8,128)S(1)} collective-permute-done((f32[3,136,128]{2,1,0:T(8,128)}, f32[3,136,128]{2,1,0:T(8,128)S(1)}, u32[]{:S(2)}, u32[]{:S(2)}) %collective-permute-start.4) | collective-permute-done | bytes 208928 | tf_op jit(solution)/shard_map/ppermute | solution.py:659
  12.8 0.0 collective-permute-start.5
  12.8 3.6 %collective-permute-done.2.refs_5_ = f32[3,136,128]{2,1,0:T(8,128)S(1)} collective-permute-done((f32[3,136,128]{2,1,0:T(8,128)}, f32[3,136,128]{2,1,0:T(8,128)S(1)}, u32[]{:S(2)}, u32[]{:S(2)}) %collective-permute-start.2) | collective-permute-done | bytes 208928 | tf_op jit(solution)/shard_map/ppermute | solution.py:659
  16.4 0.0 collective-permute-start.3
  16.4 0.3 collective-permute-done.refs_3_
  16.7 0.2 collective-permute-start.1
  16.9 0.7 pad_maximum_fusion
  17.7 2.8 %collective-permute-start.6 = (f32[12,8,128]{2,1,0:T(8,128)S(1)}, f32[12,8,128]{2,1,0:T(8,128)S(1)}, u32[]{:S(2)}, u32[]{:S(2)}) collective-permute-start(f32[12,8,128]{2,1,0:T(8,128)S(1)} %pad_maximum_fusion), channel_id=1, source_target_pairs={{0,4},{4,0},{1,5},{5,1},{2,6},{6,2},{3,7},{7,3},{8,12},{12,8},{9,1... | collective-permute-start | bytes 147464 | tf_op jit(solution)/shard_map/ppermute | solution.py:666
  20.4 2.7 %collective-permute-done.6.refs_9_ = f32[12,8,128]{2,1,0:T(8,128)S(1)} collective-permute-done((f32[12,8,128]{2,1,0:T(8,128)S(1)}, f32[12,8,128]{2,1,0:T(8,128)S(1)}, u32[]{:S(2)}, u32[]{:S(2)}) %collective-permute-start.6) | collective-permute-done | bytes 49184 | tf_op jit(solution)/shard_map/ppermute | solution.py:666
  23.2 0.0 collective-permute-done.5.refs_8_
  23.2 0.0 collective-permute-done.3.refs_6_
  23.2 0.0 copy-start.5
  23.2 0.0 collective-permute-done.1.refs_4_
  23.2 0.0 copy-start.6
  23.2 0.0 copy-done.1
  23.2 0.0 copy-done.2
  23.3 0.5 copy-done.7
  23.8 0.1 copy-done.4
  23.9 0.1 copy-done.5
  24.0 0.1 copy-done.6
  24.0 39.7 %solve_retarded.1 = (f32[4,4,4,3,8,128]{5,4,3,2,1,0:T(8,128)}, f32[48,1,128]{2,1,0:T(1,128)}, f32[48,64,128]{2,1,0:T(8,128)}, f32[48,64,128]{2,1,0:T(8,128)}, f3...) custom-call(s32[4]{0:T(128)} %pad_add_fusion.where_ref, ...), custom_call_target="tpu_custom_call" | custom-call | tf_op jit(solution)/shard_map/solve_retarded/pallas_call | solution.py:559
  63.7 3.8 %all-to-all-start = ((f32[16,4,3,8,128]{4,3,2,1,0:T(8,128)}), f32[16,4,3,8,128]{4,3,2,1,0:T(8,128)S(1)}, u32[]{:S(2)}, u32[]{:S(2)}) async-start(f32[16,4,3,8,128]{4,3,2,1,0:T(8,128)} %bitcast.9), calls=%async_computation | async-start | bytes 1572864 | tf_op jit(solution)/shard_map/all_to_all | solution.py:672
  67.5 16.0 %solve_lesser.1 = f32[4,4,2,4,3,8,128]{6,5,4,3,2,1,0:T(8,128)} custom-call(s32[4]{0:T(128)} %pad_add_fusion.where_ref, f32[48,1,128]{2,1,0:T(1,128)} %get-tuple-element.22.gains, f32[48,64,128]{2,1,0:T(8,128)} %get-tuple-element.23.refs_0_, f32[48,64,128]{2,1,0:T(8,128)} %get-tuple-element.24.refs_1_, f32[48,64,128]{2,1,0:T(8,128)} %get-tuple-element.25.refs_2_, ...), custom_call_target="tpu_custom_call" | custom-call | tf_op jit(solution)/shard_map/solve_lesser/pallas_call | solution.py:582
  83.5 0.0 all-to-all-done.power_ref
  83.5 27.0 %all_to_all.10.got_ref = f32[16,2,4,3,8,128]{5,4,3,2,1,0:T(8,128)} all-to-all(f32[16,2,4,3,8,128]{5,4,3,2,1,0:T(8,128)} %bitcast.8), channel_id=1, replica_groups=mesh['slab'=4,'half'=2,'line'=4] {'slab','line'}, dimensions={0} | all-to-all | bytes 3145728 | tf_op jit(solution)/shard_map/all_to_all | solution.py:672
  110.5 0.0 copy-done
  110.5 7.1 %correlate.1 = f32[2,64,3,8,128]{4,3,2,1,0:T(8,128)} custom-call(f32[16,4,3,8,128]{4,3,2,1,0:T(8,128)} %copy-done, f32[16,2,4,3,8,128]{5,4,3,2,1,0:T(8,128)} %all_to_all.10.got_ref), custom_call_target="tpu_custom_call" | custom-call | tf_op jit(solution)/shard_map/correlate/pallas_call | solution.py:627
  (10 shorter events, 0.0 us)
Async XLA Ops:
  2.7 10.1 %collective-permute-start.4 = (f32[3,136,128]{2,1,0:T(8,128)}, f32[3,136,128]{2,1,0:T(8,128)S(1)}, u32[]{:S(2)}, u32[]{:S(2)}) collective-permute-start(f32[3,136,128]{2,1,0:T(8,128)} %get-tuple-element.20), channel_id=1, source_target_pairs={{0,24},{8,16},{16,8},{24,0},{1,25},{9,17},{17,9},{25,1},{2,26},{10... | collective-permute-start | bytes 626696 | tf_op jit(solution)/shard_map/ppermute | solution.py:659
  6.6 9.9 %collective-permute-start.2 = (f32[3,136,128]{2,1,0:T(8,128)}, f32[3,136,128]{2,1,0:T(8,128)S(1)}, u32[]{:S(2)}, u32[]{:S(2)}) collective-permute-start(f32[3,136,128]{2,1,0:T(8,128)} %get-tuple-element.20), channel_id=1, source_target_pairs={{0,16},{8,24},{16,0},{24,8},{1,17},{9,25},{17,1},{25,9},{2,18},{10... | collective-permute-start | bytes 626696 | tf_op jit(solution)/shard_map/ppermute | solution.py:659
  7.1 9.6 %collective-permute-start = (f32[3,136,128]{2,1,0:T(8,128)}, f32[3,136,128]{2,1,0:T(8,128)S(1)}, u32[]{:S(2)}, u32[]{:S(2)}) collective-permute-start(f32[3,136,128]{2,1,0:T(8,128)} %get-tuple-element.20), channel_id=1, source_target_pairs={{0,8},{8,0},{16,24},{24,16},{1,9},{9,1},{17,25},{25,17},{2,10},{10... | collective-permute-start | bytes 626696 | tf_op jit(solution)/shard_map/ppermute | solution.py:659
  12.8 10.4 %copy-start.1 = (f32[3,136,128]{2,1,0:T(8,128)}, f32[3,136,128]{2,1,0:T(8,128)S(1)}, u32[]{:S(2)}) copy-start(f32[3,136,128]{2,1,0:T(8,128)S(1)} %collective-permute-done.4.refs_7_) | copy-start | bytes 626692
  12.8 10.4 %collective-permute-start.5 = (f32[3,136,128]{2,1,0:T(8,128)S(1)}, f32[3,136,128]{2,1,0:T(8,128)S(1)}, u32[]{:S(2)}, u32[]{:S(2)}) collective-permute-start(f32[3,136,128]{2,1,0:T(8,128)S(1)} %collective-permute-done.4.refs_7_), channel_id=1, source_target_pairs={{0,1},{1,0},{2,3},{3,2},{4,5},{5,4},{6,7},{7,6},{8,9},{9,8},{10,11... | collective-permute-start | bytes 626696 | tf_op jit(solution)/shard_map/ppermute | solution.py:663
  16.4 6.8 %copy-start.2 = (f32[3,136,128]{2,1,0:T(8,128)}, f32[3,136,128]{2,1,0:T(8,128)S(1)}, u32[]{:S(2)}) copy-start(f32[3,136,128]{2,1,0:T(8,128)S(1)} %collective-permute-done.2.refs_5_) | copy-start | bytes 626692
  16.4 6.8 %collective-permute-start.3 = (f32[3,136,128]{2,1,0:T(8,128)S(1)}, f32[3,136,128]{2,1,0:T(8,128)S(1)}, u32[]{:S(2)}, u32[]{:S(2)}) collective-permute-start(f32[3,136,128]{2,1,0:T(8,128)S(1)} %collective-permute-done.2.refs_5_), channel_id=1, source_target_pairs={{0,1},{1,0},{2,3},{3,2},{4,5},{5,4},{6,7},{7,6},{8,9},{9,8},{10,11... | collective-permute-start | bytes 626696 | tf_op jit(solution)/shard_map/ppermute | solution.py:663
  16.7 6.5 %copy-start.3 = (f32[3,136,128]{2,1,0:T(8,128)}, f32[3,136,128]{2,1,0:T(8,128)S(1)}, u32[]{:S(2)}) copy-start(f32[3,136,128]{2,1,0:T(8,128)S(1)} %collective-permute-done.refs_3_) | copy-start | bytes 626692
  16.7 6.5 %collective-permute-start.1 = (f32[3,136,128]{2,1,0:T(8,128)S(1)}, f32[3,136,128]{2,1,0:T(8,128)S(1)}, u32[]{:S(2)}, u32[]{:S(2)}) collective-permute-start(f32[3,136,128]{2,1,0:T(8,128)S(1)} %collective-permute-done.refs_3_), channel_id=1, source_target_pairs={{0,1},{1,0},{2,3},{3,2},{4,5},{5,4},{6,7},{7,6},{8,9},{9,8},{10,11... | collective-permute-start | bytes 626696 | tf_op jit(solution)/shard_map/ppermute | solution.py:663
  17.7 5.5 %collective-permute-start.6 = (f32[12,8,128]{2,1,0:T(8,128)S(1)}, f32[12,8,128]{2,1,0:T(8,128)S(1)}, u32[]{:S(2)}, u32[]{:S(2)}) collective-permute-start(f32[12,8,128]{2,1,0:T(8,128)S(1)} %pad_maximum_fusion), channel_id=1, source_target_pairs={{0,4},{4,0},{1,5},{5,1},{2,6},{6,2},{3,7},{7,3},{8,12},{12,8},{9,1... | collective-permute-start | bytes 147464 | tf_op jit(solution)/shard_map/ppermute | solution.py:666
  23.2 0.6 copy-start.7
  23.2 0.7 copy-start.4
  23.2 0.8 copy-start.5
  23.2 0.8 copy-start.6
  63.7 19.8 %all-to-all-start = ((f32[16,4,3,8,128]{4,3,2,1,0:T(8,128)}), f32[16,4,3,8,128]{4,3,2,1,0:T(8,128)S(1)}, u32[]{:S(2)}, u32[]{:S(2)}) async-start(f32[16,4,3,8,128]{4,3,2,1,0:T(8,128)} %bitcast.9), calls=%async_computation | async-start | bytes 1572864 | tf_op jit(solution)/shard_map/all_to_all | solution.py:672
  83.5 27.0 %copy-start = (f32[16,4,3,8,128]{4,3,2,1,0:T(8,128)}, f32[16,4,3,8,128]{4,3,2,1,0:T(8,128)S(1)}, u32[]{:S(2)}) copy-start(f32[16,4,3,8,128]{4,3,2,1,0:T(8,128)S(1)} %all-to-all-done.power_ref) | copy-start | bytes 2359300

commit v2 on v1

--- a/solution.py
+++ b/solution.py
@@ -13,7 +13,8 @@
 LEAST = 0.0095
 CLOSE = 1e-3
 STRIDE = 4
-GROUP = 8
+GROUP = 24
+ASSEMBLED = 3
 HALVES = 2
 
 
@@ -266,34 +267,45 @@
                 at = (owner ^ k) * per + i
                 data[at, 2 * width + h * local : 2 * width + (h + 1) * local, :] = others[h - 1][k * per + i]
 
-    pps, qqs = [], []
-    for s in range(slabs):
+    def assemble(s, unused):
         both = data[s, 0:width, :]
         with_p = times(both, turned(both[:orbits], 3), 1)
         with_q = times(both, turned(both[orbits:], 3), 1)
-        pps.append(with_p[:orbits])
-        qqs.append(with_q[orbits:])
-        if s > 0:
-            up1[s - 1] = -with_q[:orbits]
-            dn1[s - 1] = -with_p[orbits:]
-    largest = None
+        hold[s, 0:orbits, 0:width] = with_p[:orbits]
+        hold[s, orbits:width, 0:width] = with_q[orbits:]
+        before = jnp.maximum(s - 1, 0)
+        up1[before] = -with_q[:orbits]
+        dn1[before] = -with_p[orbits:]
+        return 0
+
+    def assemble_some(place, unused):
+        for n in range(ASSEMBLED):
+            assemble(place * ASSEMBLED + n, 0)
+        return 0
+
+    lax.fori_loop(0, slabs // ASSEMBLED, assemble_some, 0)
+    for s in range(slabs // ASSEMBLED * ASSEMBLED, slabs):
+        assemble(s, 0)
+    largest = largest_shift = None
     for s in range(slabs):
-        base = qqs[s]
+        base = hold[s, orbits:width, 0:width]
         if s + 1 < slabs:
-            base = base + pps[s + 1]
+            base = base + hold[s + 1, 0:orbits, 0:width]
         if s == 0:
-            base = base + pps[0]
+            base = base + hold[0, 0:orbits, 0:width]
+        squares = base * base
+        sums = jnp.sum(jnp.sqrt(squares + half_roll(squares)), axis=0, keepdims=True)
+        largest = sums if largest is None else jnp.maximum(largest, sums)
         for e in range(mine):
             row = 2 * width + ((e // share) ^ half) * local + first + e % share
             settings = data[s, pl.ds(row, 1), :]
             m = spot[s] * mine + e
             gains[m] = settings
-            block = base + jnp.where(diag_lane, settings, 0.0)
-            mat[m] = block
+            mat[m] = base + jnp.where(diag_lane, settings, 0.0)
             rhs[m] = data[s, width : 2 * width, :]
-            sums = jnp.sum(jnp.abs(block), axis=0, keepdims=True)
-            largest = sums if largest is None else jnp.maximum(largest, sums)
-    top = 1.01 * jnp.max(largest + half_roll(largest))
+            largest_shift = settings if largest_shift is None else jnp.maximum(largest_shift, settings)
+    shift_lane = lax.broadcasted_iota(jnp.int32, largest_shift.shape, 1) < orbits
+    top = 1.01 * jnp.max(largest + jnp.max(jnp.where(shift_lane, largest_shift, 0.0)))
     copy_out(3, 0, slabs - 1)
     copy_out(4, 0, slabs - 1)
 
@@ -388,15 +400,18 @@
 
     def finished(nodes):
         copy_out(7, spot[nodes[0]] * mine, (spot[nodes[-1]] + 1) * mine)
-        for s in nodes:
-            for e in range(mine):
-                xr, xi = orbitals_of(sol, spot[s] * mine + e, half, halves, orbits)
-                power = xr * xr + xi * xi
-                for j in range(lines):
-                    power_ref[s // per, j, e, s % per, :, :] = power[j * orb_per : (j + 1) * orb_per, :]
+
+    def deliver(e, unused):
+        for s in range(slabs):
+            xr, xi = orbitals_of(sol, spot[s] * mine + e, half, halves, orbits)
+            power = xr * xr + xi * xi
+            for j in range(lines):
+                power_ref[s // per, j, e, s % per, :, :] = power[j * orb_per : (j + 1) * orb_per, :]
+        return 0
 
     finished([root])
     climb(levels, spot, mine, w1, w2, sol, finished)
+    lax.fori_loop(0, mine, deliver, 0)
     for copy in copies:
         copy.wait()
 
@@ -444,9 +459,15 @@
     lane = lax.broadcasted_iota(jnp.int32, (orbits, width), 1)
     sub = lax.broadcasted_iota(jnp.int32, (orbits, width), 0)
     gain_lane = lane == sub + orbits
-    for m in range(slabs * mine):
-        gain = jnp.sum(jnp.where(gain_lane, gains[m], 0.0), axis=1, keepdims=True)
-        rhs[m] = wide(ret[m]) * gain
+
+    def scale(s, unused):
+        for e in range(mine):
+            m = s * mine + e
+            gain = jnp.sum(jnp.where(gain_lane, gains[m], 0.0), axis=1, keepdims=True)
+            rhs[m] = wide(ret[m]) * gain
+        return 0
+
+    lax.fori_loop(0, slabs, scale, 0)
     for depth, level in enumerate(levels):
         for which in (0, 3, 4, 5, 6):
             if (which, depth) in fetches:
@@ -484,8 +505,9 @@
         fetches[(1, depth)].wait()
         fetches[(2, depth)].wait()
     climb(levels, spot, mine, w1, w2, sol, lambda nodes: None)
-    for s in range(slabs):
-        for e in range(mine):
+
+    def deliver(e, unused):
+        for s in range(slabs):
             m = spot[s] * mine + e
             xr, xi = orbitals_of(ret, m, half, halves, orbits)
             yr, yi = orbitals_of(sol, m, half, halves, orbits)
@@ -495,6 +517,9 @@
                 rows = slice(j * orb_per, (j + 1) * orb_per)
                 out_ref[s // per, j, 0, e, s % per, :, :] = re[rows, :]
                 out_ref[s // per, j, 1, e, s % per, :, :] = im[rows, :]
+        return 0
+
+    lax.fori_loop(0, mine, deliver, 0)
 
 
 def pack_kernel(where_ref, p_ref, q_ref, src_ref, shift_ref, gain_ref, factors_ref, settings_ref, parcel_ref):

time: 118 us -> 114 us (0.966)
  Pallas kernels: 64.8 us -> 60.5 us
    pallas_call x1, Pallas kernels: 39.7 us -> 34.5 us  [solve_retarded(): pl.pallas_call(functools.partial(retarded_kernel, plan), out_shape=[jax.S...]
  transfers between devices with their start and end apart: 8 -> 8, of which waited for: 4 -> 4; matrix products, arithmetic and copies ran while one was open for 1% -> 1% of each run, Pallas kernels for 14% -> 15%
where the time goes in v2:
time: 114 us; the launch traced here: 113 us
  Pallas kernels  60.5 us (53%)
  blocking collectives  27 us (24%)
  waiting for transfers between devices  12.3 us (11%)
  starting transfers between devices  11.3 us (10%)
  other arithmetic  1.36 us (1%)
    pallas_call x1, Pallas kernels, solve_retarded(): pl.pallas_call(functools.partial(retarded_kernel, plan), out_shape=[jax.S...  34.5 us
    all_to_all x1, blocking collectives, spread(): lax.all_to_all(array, ('slab', 'line'), split_axis=0, concat_axis=0, tile...  27 us
    pallas_call x1, Pallas kernels, solve_lesser(): pl.pallas_call(functools.partial(lesser_kernel, plan), out_shape=jax.Shap...  16.8 us
    ppermute x3, waiting for transfers between devices, per_device(): lax.ppermute(parcel, 'slab', [(g, g ^ k) for g in range(groups)])  9.55 us
    pallas_call x1, Pallas kernels, correlate(): pl.pallas_call(functools.partial(correlate_kernel, order), grid=(per,), o...  7.11 us
    ppermute x3, starting transfers between devices, per_device(): lax.ppermute(parcel, 'slab', [(g, g ^ k) for g in range(groups)])  4.46 us
    all_to_all x1, starting transfers between devices, spread(): lax.all_to_all(array, ('slab', 'line'), split_axis=0, concat_axis=0, tile...  3.8 us
    ppermute x1, starting transfers between devices, per_device(): lax.ppermute(known, 'half', [(a, a ^ h) for a in range(halves)])  2.78 us
  transfers between devices with their start and end apart: 8, of which 4 were waited for; matrix products, arithmetic and copies ran while one was open for 1% of the time, Pallas kernels for 15%

profile of v2, /device:TPU:0, one launch (start us, length us, event | category | flops | bytes accessed | tf_op | source)
XLA Modules:
  0.0 113.3 jit_solution(607936145850761184)
XLA Ops:
  0.0 0.7 pad_add_fusion.where_ref
  0.7 2.0 %pack_parcel.1 = (f32[3,128,128]{2,1,0:T(8,128)}, f32[3,8,128]{2,1,0:T(8,128)}, f32[3,136,128]{2,1,0:T(8,128)}) custom-call(s32[4]{0:T(128)} %pad_add_fusion.where_ref, f32[3,2,64,64]{3,2,1,0:T(8,128)} %p_ref.1, f32[3,2,64,64]{3,2,1,0:T(8,128)} %q_ref.1, f32[3,2,64,128]{3,2,1,0:T(8,128)} %refs_1_.1, f32[3,8,64]{2,1,0:T(8,128)} %bitcast.10, f32[3,8,64]{2,1,0:T(8,128)} %bitcast.11), custom_call_target="tpu_custom_call" | custom-call | tf_op jit(solution)/shard_map/pack_parcel/pallas_call | solution.py:553
  2.7 3.9 %collective-permute-start.4 = (f32[3,136,128]{2,1,0:T(8,128)}, f32[3,136,128]{2,1,0:T(8,128)S(1)}, u32[]{:S(2)}, u32[]{:S(2)}) collective-permute-start(f32[3,136,128]{2,1,0:T(8,128)} %get-tuple-element.20), channel_id=1, source_target_pairs={{0,24},{8,16},{16,8},{24,0},{1,25},{9,17},{17,9},{25,1},{2,26},{10... | collective-permute-start | bytes 626696 | tf_op jit(solution)/shard_map/ppermute | solution.py:684
  6.6 0.5 collective-permute-start.2
  7.1 0.1 collective-permute-start
  7.1 5.7 %collective-permute-done.4.refs_7_ = f32[3,136,128]{2,1,0:T(8,128)S(1)} collective-permute-done((f32[3,136,128]{2,1,0:T(8,128)}, f32[3,136,128]{2,1,0:T(8,128)S(1)}, u32[]{:S(2)}, u32[]{:S(2)}) %collective-permute-start.4) | collective-permute-done | bytes 208928 | tf_op jit(solution)/shard_map/ppermute | solution.py:684
  12.8 0.0 collective-permute-start.5
  12.8 3.6 %collective-permute-done.2.refs_5_ = f32[3,136,128]{2,1,0:T(8,128)S(1)} collective-permute-done((f32[3,136,128]{2,1,0:T(8,128)}, f32[3,136,128]{2,1,0:T(8,128)S(1)}, u32[]{:S(2)}, u32[]{:S(2)}) %collective-permute-start.2) | collective-permute-done | bytes 208928 | tf_op jit(solution)/shard_map/ppermute | solution.py:684
  16.4 0.0 collective-permute-start.3
  16.4 0.3 collective-permute-done.refs_3_
  16.7 0.2 collective-permute-start.1
  16.9 0.7 pad_maximum_fusion
  17.7 2.8 %collective-permute-start.6 = (f32[12,8,128]{2,1,0:T(8,128)S(1)}, f32[12,8,128]{2,1,0:T(8,128)S(1)}, u32[]{:S(2)}, u32[]{:S(2)}) collective-permute-start(f32[12,8,128]{2,1,0:T(8,128)S(1)} %pad_maximum_fusion), channel_id=1, source_target_pairs={{0,4},{4,0},{1,5},{5,1},{2,6},{6,2},{3,7},{7,3},{8,12},{12,8},{9,1... | collective-permute-start | bytes 147464 | tf_op jit(solution)/shard_map/ppermute | solution.py:691
  20.4 2.7 %collective-permute-done.6.refs_9_ = f32[12,8,128]{2,1,0:T(8,128)S(1)} collective-permute-done((f32[12,8,128]{2,1,0:T(8,128)S(1)}, f32[12,8,128]{2,1,0:T(8,128)S(1)}, u32[]{:S(2)}, u32[]{:S(2)}) %collective-permute-start.6) | collective-permute-done | bytes 49184 | tf_op jit(solution)/shard_map/ppermute | solution.py:691
  23.2 0.0 collective-permute-done.5.refs_8_
  23.2 0.0 collective-permute-done.3.refs_6_
  23.2 0.0 copy-start.5
  23.2 0.0 collective-permute-done.1.refs_4_
  23.2 0.0 copy-start.6
  23.2 0.0 copy-done.1
  23.2 0.0 copy-done.2
  23.2 0.0 copy-done.3
  23.3 0.5 copy-done.7
  23.8 0.1 copy-done.4
  23.9 0.1 copy-done.5
  24.0 0.1 copy-done.6
  24.0 34.5 %solve_retarded.1 = (f32[4,4,4,3,8,128]{5,4,3,2,1,0:T(8,128)}, f32[48,1,128]{2,1,0:T(1,128)}, f32[48,64,128]{2,1,0:T(8,128)}, f32[48,64,128]{2,1,0:T(8,128)}, f3...) custom-call(s32[4]{0:T(128)} %pad_add_fusion.where_ref, ...), custom_call_target="tpu_custom_call" | custom-call | tf_op jit(solution)/shard_map/solve_retarded/pallas_call | solution.py:584
  58.5 3.8 %all-to-all-start = ((f32[16,4,3,8,128]{4,3,2,1,0:T(8,128)}), f32[16,4,3,8,128]{4,3,2,1,0:T(8,128)S(1)}, u32[]{:S(2)}, u32[]{:S(2)}) async-start(f32[16,4,3,8,128]{4,3,2,1,0:T(8,128)} %bitcast.9), calls=%async_computation | async-start | bytes 1572864 | tf_op jit(solution)/shard_map/all_to_all | solution.py:697
  62.4 16.8 %solve_lesser.1 = f32[4,4,2,4,3,8,128]{6,5,4,3,2,1,0:T(8,128)} custom-call(s32[4]{0:T(128)} %pad_add_fusion.where_ref, f32[48,1,128]{2,1,0:T(1,128)} %get-tuple-element.22.gains, f32[48,64,128]{2,1,0:T(8,128)} %get-tuple-element.23.refs_0_, f32[48,64,128]{2,1,0:T(8,128)} %get-tuple-element.24.refs_1_, f32[48,64,128]{2,1,0:T(8,128)} %get-tuple-element.25.refs_2_, ...), custom_call_target="tpu_custom_call" | custom-call | tf_op jit(solution)/shard_map/solve_lesser/pallas_call | solution.py:607
  79.2 0.0 all-to-all-done.power_ref
  79.2 27.0 %all_to_all.10.got_ref = f32[16,2,4,3,8,128]{5,4,3,2,1,0:T(8,128)} all-to-all(f32[16,2,4,3,8,128]{5,4,3,2,1,0:T(8,128)} %bitcast.8), channel_id=1, replica_groups=mesh['slab'=4,'half'=2,'line'=4] {'slab','line'}, dimensions={0} | all-to-all | bytes 3145728 | tf_op jit(solution)/shard_map/all_to_all | solution.py:697
  106.2 7.1 %correlate.1 = f32[2,64,3,8,128]{4,3,2,1,0:T(8,128)} custom-call(f32[16,4,3,8,128]{4,3,2,1,0:T(8,128)} %copy-done, f32[16,2,4,3,8,128]{5,4,3,2,1,0:T(8,128)} %all_to_all.10.got_ref), custom_call_target="tpu_custom_call" | custom-call | tf_op jit(solution)/shard_map/correlate/pallas_call | solution.py:652
  (10 shorter events, 0.0 us)
Async XLA Ops:
  2.7 10.1 %collective-permute-start.4 = (f32[3,136,128]{2,1,0:T(8,128)}, f32[3,136,128]{2,1,0:T(8,128)S(1)}, u32[]{:S(2)}, u32[]{:S(2)}) collective-permute-start(f32[3,136,128]{2,1,0:T(8,128)} %get-tuple-element.20), channel_id=1, source_target_pairs={{0,24},{8,16},{16,8},{24,0},{1,25},{9,17},{17,9},{25,1},{2,26},{10... | collective-permute-start | bytes 626696 | tf_op jit(solution)/shard_map/ppermute | solution.py:684
  6.6 9.9 %collective-permute-start.2 = (f32[3,136,128]{2,1,0:T(8,128)}, f32[3,136,128]{2,1,0:T(8,128)S(1)}, u32[]{:S(2)}, u32[]{:S(2)}) collective-permute-start(f32[3,136,128]{2,1,0:T(8,128)} %get-tuple-element.20), channel_id=1, source_target_pairs={{0,16},{8,24},{16,0},{24,8},{1,17},{9,25},{17,1},{25,9},{2,18},{10... | collective-permute-start | bytes 626696 | tf_op jit(solution)/shard_map/ppermute | solution.py:684
  7.1 9.6 %collective-permute-start = (f32[3,136,128]{2,1,0:T(8,128)}, f32[3,136,128]{2,1,0:T(8,128)S(1)}, u32[]{:S(2)}, u32[]{:S(2)}) collective-permute-start(f32[3,136,128]{2,1,0:T(8,128)} %get-tuple-element.20), channel_id=1, source_target_pairs={{0,8},{8,0},{16,24},{24,16},{1,9},{9,1},{17,25},{25,17},{2,10},{10... | collective-permute-start | bytes 626696 | tf_op jit(solution)/shard_map/ppermute | solution.py:684
  12.8 10.4 %copy-start.1 = (f32[3,136,128]{2,1,0:T(8,128)}, f32[3,136,128]{2,1,0:T(8,128)S(1)}, u32[]{:S(2)}) copy-start(f32[3,136,128]{2,1,0:T(8,128)S(1)} %collective-permute-done.4.refs_7_) | copy-start | bytes 626692
  12.8 10.4 %collective-permute-start.5 = (f32[3,136,128]{2,1,0:T(8,128)S(1)}, f32[3,136,128]{2,1,0:T(8,128)S(1)}, u32[]{:S(2)}, u32[]{:S(2)}) collective-permute-start(f32[3,136,128]{2,1,0:T(8,128)S(1)} %collective-permute-done.4.refs_7_), channel_id=1, source_target_pairs={{0,1},{1,0},{2,3},{3,2},{4,5},{5,4},{6,7},{7,6},{8,9},{9,8},{10,11... | collective-permute-start | bytes 626696 | tf_op jit(solution)/shard_map/ppermute | solution.py:688
  16.4 6.8 %copy-start.2 = (f32[3,136,128]{2,1,0:T(8,128)}, f32[3,136,128]{2,1,0:T(8,128)S(1)}, u32[]{:S(2)}) copy-start(f32[3,136,128]{2,1,0:T(8,128)S(1)} %collective-permute-done.2.refs_5_) | copy-start | bytes 626692
  16.4 6.8 %collective-permute-start.3 = (f32[3,136,128]{2,1,0:T(8,128)S(1)}, f32[3,136,128]{2,1,0:T(8,128)S(1)}, u32[]{:S(2)}, u32[]{:S(2)}) collective-permute-start(f32[3,136,128]{2,1,0:T(8,128)S(1)} %collective-permute-done.2.refs_5_), channel_id=1, source_target_pairs={{0,1},{1,0},{2,3},{3,2},{4,5},{5,4},{6,7},{7,6},{8,9},{9,8},{10,11... | collective-permute-start | bytes 626696 | tf_op jit(solution)/shard_map/ppermute | solution.py:688
  16.7 6.5 %copy-start.3 = (f32[3,136,128]{2,1,0:T(8,128)}, f32[3,136,128]{2,1,0:T(8,128)S(1)}, u32[]{:S(2)}) copy-start(f32[3,136,128]{2,1,0:T(8,128)S(1)} %collective-permute-done.refs_3_) | copy-start | bytes 626692
  16.7 6.5 %collective-permute-start.1 = (f32[3,136,128]{2,1,0:T(8,128)S(1)}, f32[3,136,128]{2,1,0:T(8,128)S(1)}, u32[]{:S(2)}, u32[]{:S(2)}) collective-permute-start(f32[3,136,128]{2,1,0:T(8,128)S(1)} %collective-permute-done.refs_3_), channel_id=1, source_target_pairs={{0,1},{1,0},{2,3},{3,2},{4,5},{5,4},{6,7},{7,6},{8,9},{9,8},{10,11... | collective-permute-start | bytes 626696 | tf_op jit(solution)/shard_map/ppermute | solution.py:688
  17.7 5.5 %collective-permute-start.6 = (f32[12,8,128]{2,1,0:T(8,128)S(1)}, f32[12,8,128]{2,1,0:T(8,128)S(1)}, u32[]{:S(2)}, u32[]{:S(2)}) collective-permute-start(f32[12,8,128]{2,1,0:T(8,128)S(1)} %pad_maximum_fusion), channel_id=1, source_target_pairs={{0,4},{4,0},{1,5},{5,1},{2,6},{6,2},{3,7},{7,3},{8,12},{12,8},{9,1... | collective-permute-start | bytes 147464 | tf_op jit(solution)/shard_map/ppermute | solution.py:691
  23.2 0.6 copy-start.7
  23.2 0.7 copy-start.4
  23.2 0.8 copy-start.5
  23.2 0.8 copy-start.6
  58.5 20.6 %all-to-all-start = ((f32[16,4,3,8,128]{4,3,2,1,0:T(8,128)}), f32[16,4,3,8,128]{4,3,2,1,0:T(8,128)S(1)}, u32[]{:S(2)}, u32[]{:S(2)}) async-start(f32[16,4,3,8,128]{4,3,2,1,0:T(8,128)} %bitcast.9), calls=%async_computation | async-start | bytes 1572864 | tf_op jit(solution)/shard_map/all_to_all | solution.py:697
  79.2 27.0 %copy-start = (f32[16,4,3,8,128]{4,3,2,1,0:T(8,128)}, f32[16,4,3,8,128]{4,3,2,1,0:T(8,128)S(1)}, u32[]{:S(2)}) copy-start(f32[16,4,3,8,128]{4,3,2,1,0:T(8,128)S(1)} %all-to-all-done.power_ref) | copy-start | bytes 2359300

commit v3 on v2

--- a/solution.py
+++ b/solution.py
@@ -475,7 +475,7 @@
 
         def work(energies, depth=depth, level=level):
             items = [(node, left, right, e) for node, left, right in level for e in energies]
-            steps = [times(inv[spot[node] * mine + e], turned(rhs[spot[node] * mine + e], 3)) for node, _, _, e in items]
+            steps = [times(inv[spot[node] * mine + e], turned(rhs[spot[node] * mine + e], 2)) for node, _, _, e in items]
             changes = []
             for (node, left, right, e), step in zip(items, steps):
                 sides = []
@@ -486,7 +486,7 @@
                     basic, place = places[(depth, node, right, 0)]
                     sides.append(dn1[place] if basic else dn2[place + e])
                 sides = sides[0] if len(sides) == 1 else jnp.concatenate(sides, axis=0)
-                changes.append(times(sides, turned(step, 3)))
+                changes.append(times(sides, turned(step, 2)))
             for (node, left, right, e), step, change in zip(items, steps, changes):
                 sol[spot[node] * mine + e] = tall(step)
                 if left is not None:
@@ -500,7 +500,7 @@
     fetches[(0, len(levels))].wait()
     for e in range(mine):
         m = spot[root] * mine + e
-        sol[m] = tall(times(inv[m], turned(rhs[m], 3)))
+        sol[m] = tall(times(inv[m], turned(rhs[m], 2)))
     for depth in range(len(levels)):
         fetches[(1, depth)].wait()
         fetches[(2, depth)].wait()

time: 114 us -> 111 us (0.974)
  Pallas kernels: 60.5 us -> 57.9 us
    pallas_call x1, Pallas kernels: 16.8 us -> 14.3 us  [solve_lesser(): pl.pallas_call(functools.partial(lesser_kernel, plan), out_shape=jax.Shap...]
  transfers between devices with their start and end apart: 8 -> 8, of which waited for: 4 -> 4; matrix products, arithmetic and copies ran while one was open for 1% -> 1% of each run, Pallas kernels for 15% -> 13%
where the time goes in v3:
time: 111 us
  Pallas kernels  57.9 us (52%)
  blocking collectives  27 us (24%)
  waiting for transfers between devices  12.3 us (11%)
  starting transfers between devices  11.3 us (10%)
  other arithmetic  1.36 us (1%)
    pallas_call x1, Pallas kernels, solve_retarded(): pl.pallas_call(functools.partial(retarded_kernel, plan), out_shape=[jax.S...  34.5 us
    all_to_all x1, blocking collectives, spread(): lax.all_to_all(array, ('slab', 'line'), split_axis=0, concat_axis=0, tile...  27 us
    pallas_call x1, Pallas kernels, solve_lesser(): pl.pallas_call(functools.partial(lesser_kernel, plan), out_shape=jax.Shap...  14.3 us
    ppermute x3, waiting for transfers between devices, per_device(): lax.ppermute(parcel, 'slab', [(g, g ^ k) for g in range(groups)])  9.55 us
    pallas_call x1, Pallas kernels, correlate(): pl.pallas_call(functools.partial(correlate_kernel, order), grid=(per,), o...  7.11 us
    ppermute x3, starting transfers between devices, per_device(): lax.ppermute(parcel, 'slab', [(g, g ^ k) for g in range(groups)])  4.46 us
    all_to_all x1, starting transfers between devices, spread(): lax.all_to_all(array, ('slab', 'line'), split_axis=0, concat_axis=0, tile...  3.8 us
    ppermute x1, starting transfers between devices, per_device(): lax.ppermute(known, 'half', [(a, a ^ h) for a in range(halves)])  2.78 us
  transfers between devices with their start and end apart: 8, of which 4 were waited for; matrix products, arithmetic and copies ran while one was open for 1% of the time, Pallas kernels for 13%

profile of v3, /device:TPU:0, one launch (start us, length us, event | category | flops | bytes accessed | tf_op | source)
XLA Modules:
  0.0 110.8 jit_solution(2583385724627722971)
XLA Ops:
  0.0 0.7 pad_add_fusion.where_ref
  0.7 2.0 %pack_parcel.1 = (f32[3,128,128]{2,1,0:T(8,128)}, f32[3,8,128]{2,1,0:T(8,128)}, f32[3,136,128]{2,1,0:T(8,128)}) custom-call(s32[4]{0:T(128)} %pad_add_fusion.where_ref, f32[3,2,64,64]{3,2,1,0:T(8,128)} %p_ref.1, f32[3,2,64,64]{3,2,1,0:T(8,128)} %q_ref.1, f32[3,2,64,128]{3,2,1,0:T(8,128)} %refs_1_.1, f32[3,8,64]{2,1,0:T(8,128)} %bitcast.10, f32[3,8,64]{2,1,0:T(8,128)} %bitcast.11), custom_call_target="tpu_custom_call" | custom-call | tf_op jit(solution)/shard_map/pack_parcel/pallas_call | solution.py:553
  2.7 3.9 %collective-permute-start.4 = (f32[3,136,128]{2,1,0:T(8,128)}, f32[3,136,128]{2,1,0:T(8,128)S(1)}, u32[]{:S(2)}, u32[]{:S(2)}) collective-permute-start(f32[3,136,128]{2,1,0:T(8,128)} %get-tuple-element.20), channel_id=1, source_target_pairs={{0,24},{8,16},{16,8},{24,0},{1,25},{9,17},{17,9},{25,1},{2,26},{10... | collective-permute-start | bytes 626696 | tf_op jit(solution)/shard_map/ppermute | solution.py:684
  6.6 0.5 collective-permute-start.2
  7.1 0.1 collective-permute-start
  7.1 5.7 %collective-permute-done.4.refs_7_ = f32[3,136,128]{2,1,0:T(8,128)S(1)} collective-permute-done((f32[3,136,128]{2,1,0:T(8,128)}, f32[3,136,128]{2,1,0:T(8,128)S(1)}, u32[]{:S(2)}, u32[]{:S(2)}) %collective-permute-start.4) | collective-permute-done | bytes 208928 | tf_op jit(solution)/shard_map/ppermute | solution.py:684
  12.8 0.0 collective-permute-start.5
  12.8 3.6 %collective-permute-done.2.refs_5_ = f32[3,136,128]{2,1,0:T(8,128)S(1)} collective-permute-done((f32[3,136,128]{2,1,0:T(8,128)}, f32[3,136,128]{2,1,0:T(8,128)S(1)}, u32[]{:S(2)}, u32[]{:S(2)}) %collective-permute-start.2) | collective-permute-done | bytes 208928 | tf_op jit(solution)/shard_map/ppermute | solution.py:684
  16.4 0.0 collective-permute-start.3
  16.4 0.3 collective-permute-done.refs_3_
  16.7 0.2 collective-permute-start.1
  16.9 0.7 pad_maximum_fusion
  17.7 2.8 %collective-permute-start.6 = (f32[12,8,128]{2,1,0:T(8,128)S(1)}, f32[12,8,128]{2,1,0:T(8,128)S(1)}, u32[]{:S(2)}, u32[]{:S(2)}) collective-permute-start(f32[12,8,128]{2,1,0:T(8,128)S(1)} %pad_maximum_fusion), channel_id=1, source_target_pairs={{0,4},{4,0},{1,5},{5,1},{2,6},{6,2},{3,7},{7,3},{8,12},{12,8},{9,1... | collective-permute-start | bytes 147464 | tf_op jit(solution)/shard_map/ppermute | solution.py:691
  20.4 2.7 %collective-permute-done.6.refs_9_ = f32[12,8,128]{2,1,0:T(8,128)S(1)} collective-permute-done((f32[12,8,128]{2,1,0:T(8,128)S(1)}, f32[12,8,128]{2,1,0:T(8,128)S(1)}, u32[]{:S(2)}, u32[]{:S(2)}) %collective-permute-start.6) | collective-permute-done | bytes 49184 | tf_op jit(solution)/shard_map/ppermute | solution.py:691
  23.2 0.0 collective-permute-done.5.refs_8_
  23.2 0.0 collective-permute-done.3.refs_6_
  23.2 0.0 collective-permute-done.1.refs_4_
  23.2 0.0 copy-start.6
  23.2 0.0 copy-done.1
  23.2 0.0 copy-done.2
  23.2 0.0 copy-done.3
  23.3 0.5 copy-done.7
  23.8 0.1 copy-done.4
  23.9 0.1 copy-done.5
  24.0 0.1 copy-done.6
  24.0 34.5 %solve_retarded.1 = (f32[4,4,4,3,8,128]{5,4,3,2,1,0:T(8,128)}, f32[48,1,128]{2,1,0:T(1,128)}, f32[48,64,128]{2,1,0:T(8,128)}, f32[48,64,128]{2,1,0:T(8,128)}, f3...) custom-call(s32[4]{0:T(128)} %pad_add_fusion.where_ref, ...), custom_call_target="tpu_custom_call" | custom-call | tf_op jit(solution)/shard_map/solve_retarded/pallas_call | solution.py:584
  58.5 3.8 %all-to-all-start = ((f32[16,4,3,8,128]{4,3,2,1,0:T(8,128)}), f32[16,4,3,8,128]{4,3,2,1,0:T(8,128)S(1)}, u32[]{:S(2)}, u32[]{:S(2)}) async-start(f32[16,4,3,8,128]{4,3,2,1,0:T(8,128)} %bitcast.9), calls=%async_computation | async-start | bytes 1572864 | tf_op jit(solution)/shard_map/all_to_all | solution.py:697
  62.4 14.3 %solve_lesser.1 = f32[4,4,2,4,3,8,128]{6,5,4,3,2,1,0:T(8,128)} custom-call(s32[4]{0:T(128)} %pad_add_fusion.where_ref, f32[48,1,128]{2,1,0:T(1,128)} %get-tuple-element.22.gains, f32[48,64,128]{2,1,0:T(8,128)} %get-tuple-element.23.refs_0_, f32[48,64,128]{2,1,0:T(8,128)} %get-tuple-element.24.refs_1_, f32[48,64,128]{2,1,0:T(8,128)} %get-tuple-element.25.refs_2_, ...), custom_call_target="tpu_custom_call" | custom-call | tf_op jit(solution)/shard_map/solve_lesser/pallas_call | solution.py:607
  76.6 0.0 all-to-all-done.power_ref
  76.6 27.0 %all_to_all.10.got_ref = f32[16,2,4,3,8,128]{5,4,3,2,1,0:T(8,128)} all-to-all(f32[16,2,4,3,8,128]{5,4,3,2,1,0:T(8,128)} %bitcast.8), channel_id=1, replica_groups=mesh['slab'=4,'half'=2,'line'=4] {'slab','line'}, dimensions={0} | all-to-all | bytes 3145728 | tf_op jit(solution)/shard_map/all_to_all | solution.py:697
  103.7 0.0 copy-done
  103.7 7.1 %correlate.1 = f32[2,64,3,8,128]{4,3,2,1,0:T(8,128)} custom-call(f32[16,4,3,8,128]{4,3,2,1,0:T(8,128)} %copy-done, f32[16,2,4,3,8,128]{5,4,3,2,1,0:T(8,128)} %all_to_all.10.got_ref), custom_call_target="tpu_custom_call" | custom-call | tf_op jit(solution)/shard_map/correlate/pallas_call | solution.py:652
  (10 shorter events, 0.0 us)
Async XLA Ops:
  2.7 10.1 %collective-permute-start.4 = (f32[3,136,128]{2,1,0:T(8,128)}, f32[3,136,128]{2,1,0:T(8,128)S(1)}, u32[]{:S(2)}, u32[]{:S(2)}) collective-permute-start(f32[3,136,128]{2,1,0:T(8,128)} %get-tuple-element.20), channel_id=1, source_target_pairs={{0,24},{8,16},{16,8},{24,0},{1,25},{9,17},{17,9},{25,1},{2,26},{10... | collective-permute-start | bytes 626696 | tf_op jit(solution)/shard_map/ppermute | solution.py:684
  6.6 9.9 %collective-permute-start.2 = (f32[3,136,128]{2,1,0:T(8,128)}, f32[3,136,128]{2,1,0:T(8,128)S(1)}, u32[]{:S(2)}, u32[]{:S(2)}) collective-permute-start(f32[3,136,128]{2,1,0:T(8,128)} %get-tuple-element.20), channel_id=1, source_target_pairs={{0,16},{8,24},{16,0},{24,8},{1,17},{9,25},{17,1},{25,9},{2,18},{10... | collective-permute-start | bytes 626696 | tf_op jit(solution)/shard_map/ppermute | solution.py:684
  7.1 9.6 %collective-permute-start = (f32[3,136,128]{2,1,0:T(8,128)}, f32[3,136,128]{2,1,0:T(8,128)S(1)}, u32[]{:S(2)}, u32[]{:S(2)}) collective-permute-start(f32[3,136,128]{2,1,0:T(8,128)} %get-tuple-element.20), channel_id=1, source_target_pairs={{0,8},{8,0},{16,24},{24,16},{1,9},{9,1},{17,25},{25,17},{2,10},{10... | collective-permute-start | bytes 626696 | tf_op jit(solution)/shard_map/ppermute | solution.py:684
  12.8 10.4 %copy-start.1 = (f32[3,136,128]{2,1,0:T(8,128)}, f32[3,136,128]{2,1,0:T(8,128)S(1)}, u32[]{:S(2)}) copy-start(f32[3,136,128]{2,1,0:T(8,128)S(1)} %collective-permute-done.4.refs_7_) | copy-start | bytes 626692
  12.8 10.4 %collective-permute-start.5 = (f32[3,136,128]{2,1,0:T(8,128)S(1)}, f32[3,136,128]{2,1,0:T(8,128)S(1)}, u32[]{:S(2)}, u32[]{:S(2)}) collective-permute-start(f32[3,136,128]{2,1,0:T(8,128)S(1)} %collective-permute-done.4.refs_7_), channel_id=1, source_target_pairs={{0,1},{1,0},{2,3},{3,2},{4,5},{5,4},{6,7},{7,6},{8,9},{9,8},{10,11... | collective-permute-start | bytes 626696 | tf_op jit(solution)/shard_map/ppermute | solution.py:688
  16.4 6.8 %copy-start.2 = (f32[3,136,128]{2,1,0:T(8,128)}, f32[3,136,128]{2,1,0:T(8,128)S(1)}, u32[]{:S(2)}) copy-start(f32[3,136,128]{2,1,0:T(8,128)S(1)} %collective-permute-done.2.refs_5_) | copy-start | bytes 626692
  16.4 6.8 %collective-permute-start.3 = (f32[3,136,128]{2,1,0:T(8,128)S(1)}, f32[3,136,128]{2,1,0:T(8,128)S(1)}, u32[]{:S(2)}, u32[]{:S(2)}) collective-permute-start(f32[3,136,128]{2,1,0:T(8,128)S(1)} %collective-permute-done.2.refs_5_), channel_id=1, source_target_pairs={{0,1},{1,0},{2,3},{3,2},{4,5},{5,4},{6,7},{7,6},{8,9},{9,8},{10,11... | collective-permute-start | bytes 626696 | tf_op jit(solution)/shard_map/ppermute | solution.py:688
  16.7 6.5 %copy-start.3 = (f32[3,136,128]{2,1,0:T(8,128)}, f32[3,136,128]{2,1,0:T(8,128)S(1)}, u32[]{:S(2)}) copy-start(f32[3,136,128]{2,1,0:T(8,128)S(1)} %collective-permute-done.refs_3_) | copy-start | bytes 626692
  16.7 6.5 %collective-permute-start.1 = (f32[3,136,128]{2,1,0:T(8,128)S(1)}, f32[3,136,128]{2,1,0:T(8,128)S(1)}, u32[]{:S(2)}, u32[]{:S(2)}) collective-permute-start(f32[3,136,128]{2,1,0:T(8,128)S(1)} %collective-permute-done.refs_3_), channel_id=1, source_target_pairs={{0,1},{1,0},{2,3},{3,2},{4,5},{5,4},{6,7},{7,6},{8,9},{9,8},{10,11... | collective-permute-start | bytes 626696 | tf_op jit(solution)/shard_map/ppermute | solution.py:688
  17.7 5.5 %collective-permute-start.6 = (f32[12,8,128]{2,1,0:T(8,128)S(1)}, f32[12,8,128]{2,1,0:T(8,128)S(1)}, u32[]{:S(2)}, u32[]{:S(2)}) collective-permute-start(f32[12,8,128]{2,1,0:T(8,128)S(1)} %pad_maximum_fusion), channel_id=1, source_target_pairs={{0,4},{4,0},{1,5},{5,1},{2,6},{6,2},{3,7},{7,3},{8,12},{12,8},{9,1... | collective-permute-start | bytes 147464 | tf_op jit(solution)/shard_map/ppermute | solution.py:691
  23.2 0.6 copy-start.7
  23.2 0.7 copy-start.4
  23.2 0.8 copy-start.5
  23.2 0.8 copy-start.6
  58.5 18.1 %all-to-all-start = ((f32[16,4,3,8,128]{4,3,2,1,0:T(8,128)}), f32[16,4,3,8,128]{4,3,2,1,0:T(8,128)S(1)}, u32[]{:S(2)}, u32[]{:S(2)}) async-start(f32[16,4,3,8,128]{4,3,2,1,0:T(8,128)} %bitcast.9), calls=%async_computation | async-start | bytes 1572864 | tf_op jit(solution)/shard_map/all_to_all | solution.py:697
  76.6 27.0 %copy-start = (f32[16,4,3,8,128]{4,3,2,1,0:T(8,128)}, f32[16,4,3,8,128]{4,3,2,1,0:T(8,128)S(1)}, u32[]{:S(2)}) copy-start(f32[16,4,3,8,128]{4,3,2,1,0:T(8,128)S(1)} %all-to-all-done.power_ref) | copy-start | bytes 2359300
